TPU v7x, 32 devices: a whole 2x2x4 slice. The times are simulated.
32 devices in a mesh: dp: 4 (over y, x), tensor: 8 (over z, core).
Axes of the slice: x: 2, y: 2, z: 4, core: 2. Of those that a mesh axis runs over, the one named last changes fastest.
Arguments:
- hidden: bfloat16 [512, 8192], P('dp', 'tensor')
- norm_gain: float32 [8192], P('tensor'), may hold values from 0.5 to 1.5
- head: bfloat16 [8192, 36864], P(None, ('dp', 'tensor'))
- targets: int32 [512], P('dp'), may hold values from 0 to 36863
- old_logprob: float32 [512], P('dp'), may hold values from -20 to -1
- lengths: int32 [4], P('dp'), may hold values from 1 to 128, as said below
Outputs:
- new_logprob: float32 [512], P('dp')
- log_ratio: float32 [512], P('dp')
Inputs may be any that keep to these rules, and one draw needn't show every extreme that they name: `lengths`: every length is at least 1 and at most 128; some sequence has 128 live tokens and some has 1.
All inputs are finite; a program needn't handle non-finite values.
Results may differ from a plain program's by a relative error of at most 0.00094.
Values may be sent and summed in bfloat16 or wider, within the bound.
No kernel may reach another device: no remote copies, remote signals or barrier semaphores. Data moves between devices by JAX's collectives and lax.ppermute only.
A program may use at most 128 MiB of HBM per device.

v0:
```python
import functools

import jax
import jax.numpy as jnp
from jax import lax
from jax.experimental import pallas as pl
from jax.experimental.pallas import tpu as pltpu
from jax.sharding import PartitionSpec as P

D = 8192
CORES = 2
X_ONLY, Y_ONLY = (0, 1), (1, 0)
VMEM_LIMIT = 16 * 1024 * 1024
LOAD_LIMIT = 36 * 1024 * 1024
SMALL_LIMIT = 6 * 1024 * 1024
EXTRA = 16
BASE = 128


class Grid:
    def __init__(self, n_dp, n_t):
        self.n_t = n_t
        self.cols = 2
        self.rows = n_dp // self.cols
        self.depth = n_t // CORES
        self.square = self.rows == self.cols
        self.first = (X_ONLY, Y_ONLY) if self.square else (X_ONLY, X_ONLY)
        self.second = (Y_ONLY, X_ONLY) if self.square else (Y_ONLY, Y_ONLY)
        self.spots = [(j, i) for j in range(self.rows) for i in range(self.cols)]

    def permute(self, a, place):
        perm = []
        for y in range(self.rows):
            for x in range(self.cols):
                for z in range(self.depth):
                    for c in range(CORES):
                        src = (y * self.cols + x) * self.n_t + z * CORES + c
                        v, u, w, d = place(y, x, z, c)
                        dst = (v % self.rows * self.cols + u % self.cols) * self.n_t
                        perm.append((src, dst + w % self.depth * CORES + d % CORES))
        return lax.ppermute(a, ("dp", "tensor"), perm)

    def plane(self, a, ways, step):
        def place(y, x, z, c):
            return y + ways[c][0] * step, x + ways[c][1] * step, z, c

        return self.permute(a, place)

    def along(self, a, step):
        return self.permute(a, lambda y, x, z, c: (y, x, z + step, c))

    def sibling(self, a):
        return self.permute(a, lambda y, x, z, c: (y, x, z, c + 1))

    def reach(self, a):
        got = {(0, 0): a}
        for i in range(1, self.cols):
            got[0, i] = self.plane(a, self.first, i)
        for j in range(1, self.rows):
            got[j, 0] = self.plane(a, self.second, j)
        return got

    def fill(self, got):
        for j in range(1, self.rows):
            for i in range(1, self.cols):
                got[j, i] = self.plane(got[0, i], self.second, j)
        return [got[s] for s in self.spots]

    def owners(self, y, x, c):
        ways = [(self.first[k], self.second[k]) for k in range(CORES)]
        out = []
        for j, i in self.spots:
            at = [
                (y - f[0] * i - s[0] * j) % self.rows * self.cols + (x - f[1] * i - s[1] * j) % self.cols
                for f, s in ways
            ]
            out.append(jnp.where(c == 0, at[0], at[1]))
        return out

    def sibling_spot(self, k):
        j, i = self.spots[k]
        return self.spots.index((i, j)) if self.square else k


def after(a, *others):
    return lax.optimization_barrier((a, *others))[0] if others else a


def diagonal(size):
    row = lax.broadcasted_iota(jnp.int32, (size, size), 0)
    return row == lax.broadcasted_iota(jnp.int32, (size, size), 1)


def to_column(row):
    return jnp.sum(jnp.where(diagonal(row.shape[1]), row, 0.0), axis=1, keepdims=True)


def to_row(column):
    return jnp.sum(jnp.where(diagonal(column.shape[0]), column, 0.0), axis=0, keepdims=True)


def layer_kernel(n, place, layer, first, last, *refs):
    refs = list(refs)
    start_ref = refs.pop(0)
    blocks = [refs.pop(0) for _ in range(CORES * n)]
    head_ref = refs.pop(0)
    acc_ref = None if first else refs.pop(0)
    marks = [refs.pop(0) for _ in range(n)] if last else None
    out_ref, rows, acc = refs if last else (*refs, refs[0])
    tok = rows.shape[0] // n
    feat = blocks[0].shape[1]
    for c in range(CORES):
        columns = pl.ds(pl.multiple_of(start_ref[1 + c], feat), feat)
        for k in range(n):
            spot = place[k] if c else k
            part = blocks[c * n + k][layer * tok : (layer + 1) * tok, :]
            rows[spot * tok : (spot + 1) * tok, columns] = part
    offset = pl.multiple_of(start_ref[0], CORES * feat)
    weights = head_ref[pl.ds(offset, CORES * feat), :]
    product = jnp.dot(rows[...], weights, preferred_element_type=jnp.float32)
    acc[...] = product if first else acc_ref[...] + product
    if not last:
        return
    base = start_ref[1 + CORES]
    for b in range(n):
        logits = acc[b * tok : (b + 1) * tok, :]
        top = jnp.max(logits, axis=1, keepdims=True)
        total = jnp.sum(jnp.exp(logits - top), axis=1, keepdims=True)
        entry = lax.broadcasted_iota(jnp.int32, logits.shape, 1) + base
        digits = marks[b][tok : tok + EXTRA, :tok].astype(jnp.float32)
        target = (digits[0:1, :] * BASE + digits[1:2, :]) * BASE + digits[2:3, :]
        target = to_column(target).astype(jnp.int32)
        pick = jnp.sum(jnp.where(entry == target, logits, 0.0), axis=1, keepdims=True)
        spot = start_ref[2 + CORES + b]
        out_ref[spot, 0:1, :] = to_row(top)
        out_ref[spot, 1:2, :] = to_row(total)
        out_ref[spot, 2:3, :] = to_row(pick)


def layer_product(tok, starts, blocks, layer, place, head, acc, marks, last):
    n = len(place)
    feat = blocks[0].shape[1]
    vocab = head.shape[1]
    vmem = pl.BlockSpec(memory_space=pltpu.VMEM)
    first = acc is None
    logits = jax.ShapeDtypeStruct((n * tok, vocab), jnp.float32)
    operands = [starts, *blocks, head] + ([] if first else [acc]) + (marks if last else [])
    scratch = [pltpu.VMEM((n * tok, CORES * feat), jnp.bfloat16)]
    if last:
        scratch.append(pltpu.VMEM(logits.shape, jnp.float32))
    work = 2 * n * tok * CORES * feat * vocab
    return pl.pallas_call(
        functools.partial(layer_kernel, n, place, layer, first, last),
        out_shape=jax.ShapeDtypeStruct((n, 3, tok), jnp.float32) if last else logits,
        in_specs=[pl.BlockSpec(memory_space=pltpu.SMEM)] + [vmem] * (len(operands) - 1),
        out_specs=vmem,
        scratch_shapes=scratch,
        compiler_params=pltpu.CompilerParams(vmem_limit_bytes=VMEM_LIMIT),
        cost_estimate=pl.CostEstimate(
            flops=work, bytes_accessed=2 * CORES * feat * vocab, transcendentals=0
        ),
    )(*operands)


def norm_kernel(size, *refs):
    blocks, sums, gains, rest = refs[:size], refs[size : size + 2], refs[size + 2 : 2 * size + 2], refs[2 * size + 2 :]
    out_ref = rest[-1]
    tok, feat = blocks[0].shape
    scale = to_column(lax.rsqrt((sums[0][...] + sums[1][...]) / D + 1e-06))
    for j in range(size):
        part = blocks[j][...].astype(jnp.float32) * scale * gains[j][:, :feat]
        out_ref[j * tok : (j + 1) * tok, :] = part.astype(jnp.bfloat16)
    if len(rest) > 1:
        target = rest[0][...]
        row = lax.broadcasted_iota(jnp.int32, (EXTRA, tok), 0)
        digits = jnp.where(row == 0, target >> 14, jnp.where(row == 1, (target >> 7) & 127, target & 127))
        out_ref[tok:, :] = jnp.zeros((EXTRA, feat), jnp.bfloat16)
        out_ref[tok:, :tok] = digits.astype(jnp.float32).astype(jnp.bfloat16)


def normalized(blocks, sums, gains, target=None):
    tok, feat = blocks[0].shape
    operands = [*blocks, *sums, *gains] + ([] if target is None else [target])
    rows = len(blocks) * tok + (0 if target is None else EXTRA)
    return pl.pallas_call(
        functools.partial(norm_kernel, len(blocks)),
        out_shape=jax.ShapeDtypeStruct((rows, feat), jnp.bfloat16),
        in_specs=[pl.BlockSpec(memory_space=pltpu.VMEM)] * len(operands),
        out_specs=pl.BlockSpec(memory_space=pltpu.VMEM),
        compiler_params=pltpu.CompilerParams(vmem_limit_bytes=SMALL_LIMIT),
    )(*operands)


def squares_kernel(hidden_ref, gain_ref, out_ref):
    values = hidden_ref[...].astype(jnp.float32)
    feat = values.shape[1]
    out_ref[:, :feat] = gain_ref[...]
    out_ref[:, feat:] = to_row(jnp.sum(values * values, axis=1, keepdims=True))


def load_kernel(head_ref, out_ref, sem):
    copy = pltpu.make_async_copy(head_ref, out_ref, sem)
    copy.start()
    copy.wait()


def loaded(head):
    return pl.pallas_call(
        load_kernel,
        out_shape=pltpu.VMEM(head.shape, head.dtype),
        in_specs=[pl.BlockSpec(memory_space=pl.ANY)],
        out_specs=pl.BlockSpec(memory_space=pltpu.VMEM),
        scratch_shapes=[pltpu.SemaphoreType.DMA],
        compiler_params=pltpu.CompilerParams(vmem_limit_bytes=LOAD_LIMIT),
    )(head)


def body(hidden, norm_gain, head, targets, old_logprob, lengths):
    n_dp, n_t = lax.axis_size("dp"), lax.axis_size("tensor")
    grid = Grid(n_dp, n_t)
    depth = grid.depth
    tok, feat = hidden.shape
    tensor = lax.axis_index("tensor")
    z_me, c_me = tensor // CORES, tensor % CORES
    groups = [[0]] + [[d, depth - d] for d in range(1, (depth + 1) // 2)] + [[depth // 2]]
    place = [grid.sibling_spot(k) for k in range(n_dp)]

    packed = pl.pallas_call(
        squares_kernel,
        out_shape=jax.ShapeDtypeStruct((1, feat + tok), jnp.float32),
        compiler_params=pltpu.CompilerParams(vmem_limit_bytes=SMALL_LIMIT),
    )(hidden, norm_gain[None, :])
    fine = [grid.along(packed, dz) if dz else packed for dz in range(depth)]
    layers = {0: hidden}
    before = []
    for group in groups[1:]:
        for dz in group:
            layers[dz] = grid.along(after(hidden, *before), dz)
        before = [layers[dz] for dz in group]

    own_sum = sum(a[:, feat:] for a in fine)
    own_sum = after(own_sum, layers[1])
    sums = (own_sum, grid.sibling(own_sum))

    vocab_cols = head.shape[1]
    vocab_start = lax.axis_index(("dp", "tensor")) * vocab_cols
    plane = lax.axis_index("dp")
    owners = grid.owners(plane // grid.cols, plane % grid.cols, c_me)
    normed, reached = [], []
    for at, group in enumerate(groups):
        sources = [layers[dz] for dz in group]
        if at:
            sources[0] = after(sources[0], *reached[-1].values())
        gains = [fine[dz] for dz in group]
        normed.append(normalized(sources, sums, gains, None if at else targets[None, :]))
        reached.append(grid.reach(normed[-1]))
    near = loaded(after(head, *reached[0].values(), normed[1]))
    acc, marks = None, None
    for at, group in enumerate(groups):
        final = at == len(groups) - 1
        spread = grid.fill(dict(reached[at]))
        if marks is None:
            marks = spread
        blocks = spread + [grid.sibling(a) for a in spread]
        following = [] if final else [*reached[at + 1].values(), *normed[at + 2 : at + 3]]
        for layer, dz in enumerate(group):
            start = (z_me - dz) % depth * (CORES * feat)
            starts = [start] + [(c_me - dc) % CORES * feat for dc in range(CORES)] + [vocab_start] + owners
            if layer == len(group) - 1:
                blocks[0] = after(blocks[0], *following)
            last = final and layer == len(group) - 1
            acc = layer_product(tok, jnp.stack(starts), blocks, layer, place, near, acc, marks, last)

    spread_stats = jnp.broadcast_to(acc[:, None], (n_dp, n_t, 3, tok)).reshape(n_dp * n_t, 3, tok)
    parts = lax.all_to_all(spread_stats, ("dp", "tensor"), 0, 0, tiled=True)
    top = jnp.max(parts[:, 0], axis=0)
    total = jnp.sum(parts[:, 1] * jnp.exp(parts[:, 0] - top[None, :]), axis=0)
    picked = jnp.sum(parts[:, 2], axis=0)

    seq_count = lengths.shape[0]
    position = jnp.arange(tok // seq_count, dtype=jnp.int32)
    live = (position[None, :] < lengths[:, None]).reshape(-1).astype(jnp.float32)
    logprob = picked - top - jnp.log(total)
    return (live * logprob, live * (logprob - old_logprob))


def solution(mesh):
    in_specs = (
        P("dp", "tensor"),
        P("tensor"),
        P(None, ("dp", "tensor")),
        P("dp"),
        P("dp"),
        P("dp"),
    )
    out_specs = (P("dp"), P("dp"))
    return jax.shard_map(body, mesh=mesh, in_specs=in_specs, out_specs=out_specs, check_vma=False)
```

profile of v0, /device:TPU:0, one launch (start us, length us, event | category | flops | bytes accessed | tf_op | source)
XLA Modules:
  0.0 99.3 jit_solution(3161515211733631146)
XLA Ops:
  0.6 3.1 %collective-permute-start = (bf16[128,1024]{1,0:T(8,128)(2,1)}, bf16[128,1024]{1,0:T(8,128)(2,1)S(1)}, u32[]{:S(2)}, u32[]{:S(2)}) collective-permute-start(bf16[128,1024]{1,0:T(8,128)(2,1)} %refs_0_.1), channel_id=1, source_target_pairs={{0,2},{1,3},{2,4},{3,5},{4,6},{5,7},{6,0},{7,1},{8,10},{9,11},{10,... | collective-permute-start | bytes 786440 | tf_op jit(solution)/shard_map/ppermute | solution.py:41
  3.7 1.0 copy-done.10
  4.7 0.7 copy-done.22
  5.5 1.6 %collective-permute-start.3 = (f32[1,1152]{1,0:T(1,128)S(1)}, f32[1,1152]{1,0:T(1,128)S(1)}, u32[]{:S(2)}, u32[]{:S(2)}) collective-permute-start(f32[1,1152]{1,0:T(1,128)S(1)} %shard_map.77.refs_3_), channel_id=1, source_target_pairs={{0,2},{1,3},{2,4},{3,5},{4,6},{5,7},{6,0},{7,1},{8,10},{9,11},{10,... | collective-permute-start | bytes 13832 | tf_op jit(solution)/shard_map/ppermute | solution.py:41
  7.1 1.1 %collective-permute-start.4 = (f32[1,1152]{1,0:T(1,128)S(1)}, f32[1,1152]{1,0:T(1,128)S(1)}, u32[]{:S(2)}, u32[]{:S(2)}) collective-permute-start(f32[1,1152]{1,0:T(1,128)S(1)} %shard_map.77.refs_3_), channel_id=1, source_target_pairs={{0,4},{1,5},{2,6},{3,7},{4,0},{5,1},{6,2},{7,3},{8,12},{9,13},{10,... | collective-permute-start | bytes 13832 | tf_op jit(solution)/shard_map/ppermute | solution.py:41
  8.2 2.8 %collective-permute-start.5 = (f32[1,1152]{1,0:T(1,128)S(1)}, f32[1,1152]{1,0:T(1,128)S(1)}, u32[]{:S(2)}, u32[]{:S(2)}) collective-permute-start(f32[1,1152]{1,0:T(1,128)S(1)} %shard_map.77.refs_3_), channel_id=1, source_target_pairs={{0,6},{1,7},{2,0},{3,1},{4,2},{5,3},{6,4},{7,5},{8,14},{9,15},{10,... | collective-permute-start | bytes 13832 | tf_op jit(solution)/shard_map/ppermute | solution.py:41
  11.1 1.5 %collective-permute-done.3.refs_4_ = f32[1,1152]{1,0:T(1,128)S(1)} collective-permute-done((f32[1,1152]{1,0:T(1,128)S(1)}, f32[1,1152]{1,0:T(1,128)S(1)}, u32[]{:S(2)}, u32[]{:S(2)}) %collective-permute-start.3) | collective-permute-done | bytes 4640 | tf_op jit(solution)/shard_map/ppermute | solution.py:41
  12.7 1.1 %collective-permute-done.6.refs_2_.refs_3_ = f32[1,128]{1,0:T(1,128)S(1)} collective-permute-done((f32[1,128]{1,0:T(1,128)S(1)}, f32[1,128]{1,0:T(1,128)S(1)}, u32[]{:S(2)}, u32[]{:S(2)}) %collective-permute-start.6) | collective-permute-done | bytes 544 | tf_op jit(solution)/shard_map/ppermute | solution.py:41
  13.8 0.9 copy-done.11
  14.8 0.7 copy-done.23
  15.6 1.6 %collective-permute-start.7 = (bf16[144,1024]{1,0:T(8,128)(2,1)S(1)}, bf16[144,1024]{1,0:T(8,128)(2,1)S(1)}, u32[]{:S(2)}, u32[]{:S(2)}) collective-permute-start(bf16[144,1024]{1,0:T(8,128)(2,1)S(1)} %shard_map.78.refs_1_.refs_11_), channel_id=1, source_target_pairs={{0,8},{1,17},{2,10},{3,19},{4,12},{5,21},{6,14},{7,23},{8,0},{9,25... | collective-permute-start | bytes 884744 | tf_op jit(solution)/shard_map/ppermute | solution.py:41
  17.1 1.5 %collective-permute-start.8 = (bf16[144,1024]{1,0:T(8,128)(2,1)S(1)}, bf16[144,1024]{1,0:T(8,128)(2,1)S(1)}, u32[]{:S(2)}, u32[]{:S(2)}) collective-permute-start(bf16[144,1024]{1,0:T(8,128)(2,1)S(1)} %shard_map.78.refs_1_.refs_11_), channel_id=1, source_target_pairs={{0,16},{1,9},{2,18},{3,11},{4,20},{5,13},{6,22},{7,15},{8,24},{9,1... | collective-permute-start | bytes 884744 | tf_op jit(solution)/shard_map/ppermute | solution.py:41
  18.6 3.9 %collective-permute-start.1 = (bf16[128,1024]{1,0:T(8,128)(2,1)S(1)}, bf16[128,1024]{1,0:T(8,128)(2,1)S(1)}, u32[]{:S(2)}, u32[]{:S(2)}) collective-permute-start(bf16[128,1024]{1,0:T(8,128)(2,1)S(1)} %copy-done.11), channel_id=1, source_target_pairs={{0,6},{1,7},{2,0},{3,1},{4,2},{5,3},{6,4},{7,5},{8,14},{9,15},{10,... | collective-permute-start | bytes 786440 | tf_op jit(solution)/shard_map/ppermute | solution.py:41
  22.5 2.6 %collective-permute-done.7.refs_2_.refs_12_ = bf16[144,1024]{1,0:T(8,128)(2,1)S(1)} collective-permute-done((bf16[144,1024]{1,0:T(8,128)(2,1)S(1)}, bf16[144,1024]{1,0:T(8,128)(2,1)S(1)}, u32[]{:S(2)}, u32[]{:S(2)}) %collective-permute-start.7) | collective-permute-done | bytes 294944 | tf_op jit(solution)/shard_map/ppermute | solution.py:41
  25.1 2.8 %collective-permute-done.1.refs_1_ = bf16[128,1024]{1,0:T(8,128)(2,1)S(1)} collective-permute-done((bf16[128,1024]{1,0:T(8,128)(2,1)S(1)}, bf16[128,1024]{1,0:T(8,128)(2,1)S(1)}, u32[]{:S(2)}, u32[]{:S(2)}) %collective-permute-start.1) | collective-permute-done | bytes 262176 | tf_op jit(solution)/shard_map/ppermute | solution.py:41
  27.9 0.2 shard_map.79.refs_1_
  28.1 0.6 collective-permute-start.9
  28.7 0.5 collective-permute-start.10
  29.2 1.5 %collective-permute-start.23 = (bf16[144,1024]{1,0:T(8,128)(2,1)S(1)}, bf16[144,1024]{1,0:T(8,128)(2,1)S(1)}, u32[]{:S(2)}, u32[]{:S(2)}) collective-permute-start(bf16[144,1024]{1,0:T(8,128)(2,1)S(1)} %collective-permute-done.7.refs_2_.refs_12_), channel_id=1, source_target_pairs={{0,16},{1,9},{2,18},{3,11},{4,20},{5,13},{6,22},{7,15},{8,24},{9,1... | collective-permute-start | bytes 884744 | tf_op jit(solution)/shard_map/ppermute | solution.py:41
  30.7 1.3 %collective-permute-start.2 = (bf16[128,1024]{1,0:T(8,128)(2,1)}, bf16[128,1024]{1,0:T(8,128)(2,1)S(1)}, u32[]{:S(2)}, u32[]{:S(2)}) collective-permute-start(bf16[128,1024]{1,0:T(8,128)(2,1)} %refs_0_.1), channel_id=1, source_target_pairs={{0,4},{1,5},{2,6},{3,7},{4,0},{5,1},{6,2},{7,3},{8,12},{9,13},{10,... | collective-permute-start | bytes 786440 | tf_op jit(solution)/shard_map/ppermute | solution.py:41
  32.0 11.0 %collective-permute-done.9.refs_2_ = bf16[256,1024]{1,0:T(8,128)(2,1)S(1)} collective-permute-done((bf16[256,1024]{1,0:T(8,128)(2,1)S(1)}, bf16[256,1024]{1,0:T(8,128)(2,1)S(1)}, u32[]{:S(2)}, u32[]{:S(2)}) %collective-permute-start.9) | collective-permute-done | bytes 524320 | tf_op jit(solution)/shard_map/ppermute | solution.py:41
  43.0 0.5 collective-permute-start.18
  43.6 0.3 collective-permute-done.23.refs_4_.refs_14_
  43.9 0.2 collective-permute-start.26
  44.1 0.3 collective-permute-start.27
  44.6 0.7 copy-done.12
  45.4 0.5 collective-permute-start.11
  45.9 0.7 copy-done.14
  46.6 0.9 collective-permute-start.19
  47.5 0.7 copy-done.16
  48.2 0.7 copy-done.18
  48.9 0.5 collective-permute-start.21
  49.4 3.3 %collective-permute-done.11.refs_2_ = bf16[128,1024]{1,0:T(8,128)(2,1)} collective-permute-done((bf16[128,1024]{1,0:T(8,128)(2,1)S(1)}, bf16[128,1024]{1,0:T(8,128)(2,1)}, u32[]{:S(2)}, u32[]{:S(2)}) %collective-permute-start.11) | collective-permute-done | bytes 262176 | tf_op jit(solution)/shard_map/ppermute | solution.py:41
  52.7 1.5 %collective-permute-start.12 = (bf16[128,1024]{1,0:T(8,128)(2,1)S(1)}, bf16[128,1024]{1,0:T(8,128)(2,1)S(1)}, u32[]{:S(2)}, u32[]{:S(2)}) collective-permute-start(bf16[128,1024]{1,0:T(8,128)(2,1)S(1)} %shard_map.80.refs_1_), channel_id=1, source_target_pairs={{0,16},{1,9},{2,18},{3,11},{4,20},{5,13},{6,22},{7,15},{8,24},{9,1... | collective-permute-start | bytes 786440 | tf_op jit(solution)/shard_map/ppermute | solution.py:41
  54.2 0.8 collective-permute-done.18.refs_4_
  55.0 4.0 %collective-permute-done.12.refs_3_ = bf16[128,1024]{1,0:T(8,128)(2,1)S(1)} collective-permute-done((bf16[128,1024]{1,0:T(8,128)(2,1)S(1)}, bf16[128,1024]{1,0:T(8,128)(2,1)S(1)}, u32[]{:S(2)}, u32[]{:S(2)}) %collective-permute-start.12) | collective-permute-done | bytes 262176 | tf_op jit(solution)/shard_map/ppermute | solution.py:41
  59.1 1.5 %collective-permute-start.13 = (bf16[128,1024]{1,0:T(8,128)(2,1)}, bf16[128,1024]{1,0:T(8,128)(2,1)}, u32[]{:S(2)}, u32[]{:S(2)}) collective-permute-start(bf16[128,1024]{1,0:T(8,128)(2,1)} %collective-permute-done.11.refs_2_), channel_id=1, source_target_pairs={{0,16},{1,9},{2,18},{3,11},{4,20},{5,13},{6,22},{7,15},{8,24},{9,1... | collective-permute-start | bytes 786440 | tf_op jit(solution)/shard_map/ppermute | solution.py:41
  61.0 6.5 %shard_map.81.refs_9_ = bf16[8192,1152]{1,0:T(8,128)(2,1)S(1)} custom-call(bf16[8192,1152]{1,0:T(8,128)(2,1)} %head_ref), custom_call_target="tpu_custom_call" | custom-call | tf_op jit(solution)/shard_map/pallas_call | solution.py:208
  67.8 3.5 %shard_map.82.refs_10_ = f32[512,1152]{1,0:T(8,128)S(1)} custom-call(s32[8]{0:T(128)S(1)} %stack.80.refs_0_, bf16[144,1024]{1,0:T(8,128)(2,1)S(1)} %shard_map.78.refs_1_.refs_11_, bf16[144,1024]{1,0:T(8,128)(2,1)S(1)} %copy-done.1, bf16[144,1024]{1,0:T(8,128)(2,1)S(1)} %copy-done.3, bf16[144,1024]{1,0:T(8,128)(2,1)S(1)} %copy-done.6, ...), custom_call_target="tpu_custom_call" | custom-call | flops 2415919104 | bytes 4718592 | tf_op jit(solution)/shard_map/pallas_call | solution.py:152
  71.4 0.5 collective-permute-start.15
  72.0 0.4 collective-permute-start.17
  72.5 4.2 %shard_map.83.refs_10_ = f32[512,1152]{1,0:T(8,128)S(1)} custom-call(s32[8]{0:T(128)S(1)} %stack.78.refs_0_, bf16[256,1024]{1,0:T(8,128)(2,1)S(1)} %shard_map.79.refs_1_, bf16[256,1024]{1,0:T(8,128)(2,1)S(1)} %collective-permute-done.9.refs_2_, bf16[256,1024]{1,0:T(8,128)(2,1)S(1)} %collective-permute-done.10.refs_3_, ...), custom_call_target="tpu_custom_call" | custom-call | flops 2415919104 | bytes 4718592 | tf_op jit(solution)/shard_map/pallas_call | solution.py:152
  76.7 4.3 %shard_map.84.refs_10_ = f32[512,1152]{1,0:T(8,128)S(1)} custom-call(s32[8]{0:T(128)S(1)} %stack.76.refs_0_, bf16[256,1024]{1,0:T(8,128)(2,1)S(1)} %shard_map.79.refs_1_, bf16[256,1024]{1,0:T(8,128)(2,1)S(1)} %collective-permute-done.9.refs_2_, bf16[256,1024]{1,0:T(8,128)(2,1)S(1)} %collective-permute-done.10.refs_3_, ...), custom_call_target="tpu_custom_call" | custom-call | flops 2415919104 | bytes 4718592 | tf_op jit(solution)/shard_map/pallas_call | solution.py:152
  81.0 4.6 %shard_map.85 = f32[4,3,128]{2,1,0:T(4,128)S(1)} custom-call(s32[8]{0:T(128)S(1)} %stack.74.refs_0_, bf16[128,1024]{1,0:T(8,128)(2,1)S(1)} %copy-done.9, bf16[128,1024]{1,0:T(8,128)(2,1)} %collective-permute-done.11.refs_2_, bf16[128,1024]{1,0:T(8,128)(2,1)S(1)} %copy-done.21, bf16[128,1024]{1,0:T(8,128)(2,1)} %collective-permute-done.13.refs_4_, ...), custom_call_target="tpu_custom_call" | custom-call | flops 2415919104 | bytes 4718592 | tf_op jit(solution)/shard_map/pallas_call | solution.py:152
  85.6 0.6 broadcast_in_dim.8
  86.2 5.0 %all-to-all-start = ((f32[32,3,128]{2,1,0:T(4,128)}), f32[32,3,128]{2,1,0:T(4,128)S(1)}, u32[]{:S(2)}, u32[]{:S(2)}) async-start(f32[32,3,128]{2,1,0:T(4,128)} %bitcast.14), calls=%async_computation | async-start | bytes 131072 | tf_op jit(solution)/shard_map/all_to_all | solution.py:275
  91.9 6.7 %all-to-all-done = f32[32,3,128]{2,1,0:T(4,128)S(1)} async-done(((f32[32,3,128]{2,1,0:T(4,128)}), f32[32,3,128]{2,1,0:T(4,128)S(1)}, u32[]{:S(2)}, u32[]{:S(2)}) %all-to-all-start) | async-done | bytes 49184 | tf_op jit(solution)/shard_map/all_to_all | solution.py:275
  98.7 0.5 compare_select_fusion
  (80 shorter events, 1.6 us)
Async XLA Ops:
  0.6 12.0 %collective-permute-start = (bf16[128,1024]{1,0:T(8,128)(2,1)}, bf16[128,1024]{1,0:T(8,128)(2,1)S(1)}, u32[]{:S(2)}, u32[]{:S(2)}) collective-permute-start(bf16[128,1024]{1,0:T(8,128)(2,1)} %refs_0_.1), channel_id=1, source_target_pairs={{0,2},{1,3},{2,4},{3,5},{4,6},{5,7},{6,0},{7,1},{8,10},{9,11},{10,... | collective-permute-start | bytes 786440 | tf_op jit(solution)/shard_map/ppermute | solution.py:41
  3.7 1.0 copy-start.10
  5.5 7.0 %collective-permute-start.3 = (f32[1,1152]{1,0:T(1,128)S(1)}, f32[1,1152]{1,0:T(1,128)S(1)}, u32[]{:S(2)}, u32[]{:S(2)}) collective-permute-start(f32[1,1152]{1,0:T(1,128)S(1)} %shard_map.77.refs_3_), channel_id=1, source_target_pairs={{0,2},{1,3},{2,4},{3,5},{4,6},{5,7},{6,0},{7,1},{8,10},{9,11},{10,... | collective-permute-start | bytes 13832 | tf_op jit(solution)/shard_map/ppermute | solution.py:41
  7.1 5.5 %collective-permute-start.4 = (f32[1,1152]{1,0:T(1,128)S(1)}, f32[1,1152]{1,0:T(1,128)S(1)}, u32[]{:S(2)}, u32[]{:S(2)}) collective-permute-start(f32[1,1152]{1,0:T(1,128)S(1)} %shard_map.77.refs_3_), channel_id=1, source_target_pairs={{0,4},{1,5},{2,6},{3,7},{4,0},{5,1},{6,2},{7,3},{8,12},{9,13},{10,... | collective-permute-start | bytes 13832 | tf_op jit(solution)/shard_map/ppermute | solution.py:41
  8.2 4.4 %collective-permute-start.5 = (f32[1,1152]{1,0:T(1,128)S(1)}, f32[1,1152]{1,0:T(1,128)S(1)}, u32[]{:S(2)}, u32[]{:S(2)}) collective-permute-start(f32[1,1152]{1,0:T(1,128)S(1)} %shard_map.77.refs_3_), channel_id=1, source_target_pairs={{0,6},{1,7},{2,0},{3,1},{4,2},{5,3},{6,4},{7,5},{8,14},{9,15},{10,... | collective-permute-start | bytes 13832 | tf_op jit(solution)/shard_map/ppermute | solution.py:41
  12.6 1.2 %collective-permute-start.6 = (f32[1,128]{1,0:T(1,128)S(1)}, f32[1,128]{1,0:T(1,128)S(1)}, u32[]{:S(2)}, u32[]{:S(2)}) collective-permute-start(f32[1,128]{1,0:T(1,128)S(1)} %slice_add_fusion.refs_1_.refs_2_), channel_id=1, source_target_pairs={{0,1},{1,0},{2,3},{3,2},{4,5},{5,4},{6,7},{7,6},{8,9},{9,8},{10,11... | collective-permute-start | bytes 1544 | tf_op jit(solution)/shard_map/ppermute | solution.py:41
  13.8 1.0 copy-start.11
  15.6 9.5 %collective-permute-start.7 = (bf16[144,1024]{1,0:T(8,128)(2,1)S(1)}, bf16[144,1024]{1,0:T(8,128)(2,1)S(1)}, u32[]{:S(2)}, u32[]{:S(2)}) collective-permute-start(bf16[144,1024]{1,0:T(8,128)(2,1)S(1)} %shard_map.78.refs_1_.refs_11_), channel_id=1, source_target_pairs={{0,8},{1,17},{2,10},{3,19},{4,12},{5,21},{6,14},{7,23},{8,0},{9,25... | collective-permute-start | bytes 884744 | tf_op jit(solution)/shard_map/ppermute | solution.py:41
  17.1 8.0 %collective-permute-start.8 = (bf16[144,1024]{1,0:T(8,128)(2,1)S(1)}, bf16[144,1024]{1,0:T(8,128)(2,1)S(1)}, u32[]{:S(2)}, u32[]{:S(2)}) collective-permute-start(bf16[144,1024]{1,0:T(8,128)(2,1)S(1)} %shard_map.78.refs_1_.refs_11_), channel_id=1, source_target_pairs={{0,16},{1,9},{2,18},{3,11},{4,20},{5,13},{6,22},{7,15},{8,24},{9,1... | collective-permute-start | bytes 884744 | tf_op jit(solution)/shard_map/ppermute | solution.py:41
  18.6 9.3 %collective-permute-start.1 = (bf16[128,1024]{1,0:T(8,128)(2,1)S(1)}, bf16[128,1024]{1,0:T(8,128)(2,1)S(1)}, u32[]{:S(2)}, u32[]{:S(2)}) collective-permute-start(bf16[128,1024]{1,0:T(8,128)(2,1)S(1)} %copy-done.11), channel_id=1, source_target_pairs={{0,6},{1,7},{2,0},{3,1},{4,2},{5,3},{6,4},{7,5},{8,14},{9,15},{10,... | collective-permute-start | bytes 786440 | tf_op jit(solution)/shard_map/ppermute | solution.py:41
  25.1 29.9 %copy-start = (bf16[144,1024]{1,0:T(8,128)(2,1)}, bf16[144,1024]{1,0:T(8,128)(2,1)S(1)}, u32[]{:S(2)}) copy-start(bf16[144,1024]{1,0:T(8,128)(2,1)S(1)} %collective-permute-done.7.refs_2_.refs_12_) | copy-start | bytes 884740
  25.1 29.9 %copy-start.2 = (bf16[144,1024]{1,0:T(8,128)(2,1)}, bf16[144,1024]{1,0:T(8,128)(2,1)S(1)}, u32[]{:S(2)}) copy-start(bf16[144,1024]{1,0:T(8,128)(2,1)S(1)} %collective-permute-done.8.refs_3_.refs_13_) | copy-start | bytes 884740
  28.1 14.9 %collective-permute-start.9 = (bf16[256,1024]{1,0:T(8,128)(2,1)S(1)}, bf16[256,1024]{1,0:T(8,128)(2,1)S(1)}, u32[]{:S(2)}, u32[]{:S(2)}) collective-permute-start(bf16[256,1024]{1,0:T(8,128)(2,1)S(1)} %shard_map.79.refs_1_), channel_id=1, source_target_pairs={{0,8},{1,17},{2,10},{3,19},{4,12},{5,21},{6,14},{7,23},{8,0},{9,25... | collective-permute-start | bytes 1572872 | tf_op jit(solution)/shard_map/ppermute | solution.py:41
  28.7 15.4 %collective-permute-start.10 = (bf16[256,1024]{1,0:T(8,128)(2,1)S(1)}, bf16[256,1024]{1,0:T(8,128)(2,1)S(1)}, u32[]{:S(2)}, u32[]{:S(2)}) collective-permute-start(bf16[256,1024]{1,0:T(8,128)(2,1)S(1)} %shard_map.79.refs_1_), channel_id=1, source_target_pairs={{0,16},{1,9},{2,18},{3,11},{4,20},{5,13},{6,22},{7,15},{8,24},{9,1... | collective-permute-start | bytes 1572872 | tf_op jit(solution)/shard_map/ppermute | solution.py:41
  29.2 14.7 %collective-permute-start.23 = (bf16[144,1024]{1,0:T(8,128)(2,1)S(1)}, bf16[144,1024]{1,0:T(8,128)(2,1)S(1)}, u32[]{:S(2)}, u32[]{:S(2)}) collective-permute-start(bf16[144,1024]{1,0:T(8,128)(2,1)S(1)} %collective-permute-done.7.refs_2_.refs_12_), channel_id=1, source_target_pairs={{0,16},{1,9},{2,18},{3,11},{4,20},{5,13},{6,22},{7,15},{8,24},{9,1... | collective-permute-start | bytes 884744 | tf_op jit(solution)/shard_map/ppermute | solution.py:41
  30.7 12.9 %collective-permute-start.2 = (bf16[128,1024]{1,0:T(8,128)(2,1)}, bf16[128,1024]{1,0:T(8,128)(2,1)S(1)}, u32[]{:S(2)}, u32[]{:S(2)}) collective-permute-start(bf16[128,1024]{1,0:T(8,128)(2,1)} %refs_0_.1), channel_id=1, source_target_pairs={{0,4},{1,5},{2,6},{3,7},{4,0},{5,1},{6,2},{7,3},{8,12},{9,13},{10,... | collective-permute-start | bytes 786440 | tf_op jit(solution)/shard_map/ppermute | solution.py:41
  32.0 12.6 %collective-permute-start.24 = (bf16[144,1024]{1,0:T(8,128)(2,1)S(1)}, bf16[144,1024]{1,0:T(8,128)(2,1)S(1)}, u32[]{:S(2)}, u32[]{:S(2)}) collective-permute-start(bf16[144,1024]{1,0:T(8,128)(2,1)S(1)} %shard_map.78.refs_1_.refs_11_), channel_id=1, source_target_pairs={{0,1},{1,0},{2,3},{3,2},{4,5},{5,4},{6,7},{7,6},{8,9},{9,8},{10,11... | collective-permute-start | bytes 884744 | tf_op jit(solution)/shard_map/ppermute | solution.py:41
  43.0 12.0 %collective-permute-start.18 = (bf16[256,1024]{1,0:T(8,128)(2,1)S(1)}, bf16[256,1024]{1,0:T(8,128)(2,1)S(1)}, u32[]{:S(2)}, u32[]{:S(2)}) collective-permute-start(bf16[256,1024]{1,0:T(8,128)(2,1)S(1)} %collective-permute-done.9.refs_2_), channel_id=1, source_target_pairs={{0,16},{1,9},{2,18},{3,11},{4,20},{5,13},{6,22},{7,15},{8,24},{9,1... | collective-permute-start | bytes 1572872 | tf_op jit(solution)/shard_map/ppermute | solution.py:41
  43.6 2.3 %collective-permute-start.25 = (bf16[144,1024]{1,0:T(8,128)(2,1)S(1)}, bf16[144,1024]{1,0:T(8,128)(2,1)S(1)}, u32[]{:S(2)}, u32[]{:S(2)}) collective-permute-start(bf16[144,1024]{1,0:T(8,128)(2,1)S(1)} %collective-permute-done.7.refs_2_.refs_12_), channel_id=1, source_target_pairs={{0,1},{1,0},{2,3},{3,2},{4,5},{5,4},{6,7},{7,6},{8,9},{9,8},{10,11... | collective-permute-start | bytes 884744 | tf_op jit(solution)/shard_map/ppermute | solution.py:41
  43.9 15.2 %copy-start.5 = (bf16[144,1024]{1,0:T(8,128)(2,1)}, bf16[144,1024]{1,0:T(8,128)(2,1)S(1)}, u32[]{:S(2)}) copy-start(bf16[144,1024]{1,0:T(8,128)(2,1)S(1)} %collective-permute-done.23.refs_4_.refs_14_) | copy-start | bytes 884740
  43.9 3.6 %collective-permute-start.26 = (bf16[144,1024]{1,0:T(8,128)(2,1)S(1)}, bf16[144,1024]{1,0:T(8,128)(2,1)S(1)}, u32[]{:S(2)}, u32[]{:S(2)}) collective-permute-start(bf16[144,1024]{1,0:T(8,128)(2,1)S(1)} %collective-permute-done.8.refs_3_.refs_13_), channel_id=1, source_target_pairs={{0,1},{1,0},{2,3},{3,2},{4,5},{5,4},{6,7},{7,6},{8,9},{9,8},{10,11... | collective-permute-start | bytes 884744 | tf_op jit(solution)/shard_map/ppermute | solution.py:41
  44.1 4.1 %collective-permute-start.27 = (bf16[144,1024]{1,0:T(8,128)(2,1)S(1)}, bf16[144,1024]{1,0:T(8,128)(2,1)S(1)}, u32[]{:S(2)}, u32[]{:S(2)}) collective-permute-start(bf16[144,1024]{1,0:T(8,128)(2,1)S(1)} %collective-permute-done.23.refs_4_.refs_14_), channel_id=1, source_target_pairs={{0,1},{1,0},{2,3},{3,2},{4,5},{5,4},{6,7},{7,6},{8,9},{9,8},{10,11... | collective-permute-start | bytes 884744 | tf_op jit(solution)/shard_map/ppermute | solution.py:41
  44.6 16.0 %copy-start.8 = (bf16[128,1024]{1,0:T(8,128)(2,1)}, bf16[128,1024]{1,0:T(8,128)(2,1)S(1)}, u32[]{:S(2)}) copy-start(bf16[128,1024]{1,0:T(8,128)(2,1)S(1)} %shard_map.80.refs_1_) | copy-start | bytes 786436
  45.4 7.4 %collective-permute-start.11 = (bf16[128,1024]{1,0:T(8,128)(2,1)S(1)}, bf16[128,1024]{1,0:T(8,128)(2,1)}, u32[]{:S(2)}, u32[]{:S(2)}) collective-permute-start(bf16[128,1024]{1,0:T(8,128)(2,1)S(1)} %shard_map.80.refs_1_), channel_id=1, source_target_pairs={{0,8},{1,17},{2,10},{3,19},{4,12},{5,21},{6,14},{7,23},{8,0},{9,25... | collective-permute-start | bytes 786440 | tf_op jit(solution)/shard_map/ppermute | solution.py:41
  46.6 24.7 %collective-permute-start.19 = (bf16[256,1024]{1,0:T(8,128)(2,1)S(1)}, bf16[256,1024]{1,0:T(8,128)(2,1)S(1)}, u32[]{:S(2)}, u32[]{:S(2)}) collective-permute-start(bf16[256,1024]{1,0:T(8,128)(2,1)S(1)} %shard_map.79.refs_1_), channel_id=1, source_target_pairs={{0,1},{1,0},{2,3},{3,2},{4,5},{5,4},{6,7},{7,6},{8,9},{9,8},{10,11... | collective-permute-start | bytes 1572872 | tf_op jit(solution)/shard_map/ppermute | solution.py:41
  48.2 23.2 %collective-permute-start.20 = (bf16[256,1024]{1,0:T(8,128)(2,1)S(1)}, bf16[256,1024]{1,0:T(8,128)(2,1)S(1)}, u32[]{:S(2)}, u32[]{:S(2)}) collective-permute-start(bf16[256,1024]{1,0:T(8,128)(2,1)S(1)} %collective-permute-done.9.refs_2_), channel_id=1, source_target_pairs={{0,1},{1,0},{2,3},{3,2},{4,5},{5,4},{6,7},{7,6},{8,9},{9,8},{10,11... | collective-permute-start | bytes 1572872 | tf_op jit(solution)/shard_map/ppermute | solution.py:41
  48.9 23.0 %collective-permute-start.21 = (bf16[256,1024]{1,0:T(8,128)(2,1)S(1)}, bf16[256,1024]{1,0:T(8,128)(2,1)}, u32[]{:S(2)}, u32[]{:S(2)}) collective-permute-start(bf16[256,1024]{1,0:T(8,128)(2,1)S(1)} %collective-permute-done.10.refs_3_), channel_id=1, source_target_pairs={{0,1},{1,0},{2,3},{3,2},{4,5},{5,4},{6,7},{7,6},{8,9},{9,8},{10,11... | collective-permute-start | bytes 1572872 | tf_op jit(solution)/shard_map/ppermute | solution.py:41
  52.7 6.4 %collective-permute-start.12 = (bf16[128,1024]{1,0:T(8,128)(2,1)S(1)}, bf16[128,1024]{1,0:T(8,128)(2,1)S(1)}, u32[]{:S(2)}, u32[]{:S(2)}) collective-permute-start(bf16[128,1024]{1,0:T(8,128)(2,1)S(1)} %shard_map.80.refs_1_), channel_id=1, source_target_pairs={{0,16},{1,9},{2,18},{3,11},{4,20},{5,13},{6,22},{7,15},{8,24},{9,1... | collective-permute-start | bytes 786440 | tf_op jit(solution)/shard_map/ppermute | solution.py:41
  55.0 17.4 %collective-permute-start.22 = (bf16[256,1024]{1,0:T(8,128)(2,1)S(1)}, bf16[256,1024]{1,0:T(8,128)(2,1)}, u32[]{:S(2)}, u32[]{:S(2)}) collective-permute-start(bf16[256,1024]{1,0:T(8,128)(2,1)S(1)} %collective-permute-done.18.refs_4_), channel_id=1, source_target_pairs={{0,1},{1,0},{2,3},{3,2},{4,5},{5,4},{6,7},{7,6},{8,9},{9,8},{10,11... | collective-permute-start | bytes 1572872 | tf_op jit(solution)/shard_map/ppermute | solution.py:41
  59.1 1.5 %copy-start.20 = (bf16[128,1024]{1,0:T(8,128)(2,1)}, bf16[128,1024]{1,0:T(8,128)(2,1)S(1)}, u32[]{:S(2)}) copy-start(bf16[128,1024]{1,0:T(8,128)(2,1)S(1)} %collective-permute-done.12.refs_3_) | copy-start | bytes 786436
  59.1 12.9 %collective-permute-start.13 = (bf16[128,1024]{1,0:T(8,128)(2,1)}, bf16[128,1024]{1,0:T(8,128)(2,1)}, u32[]{:S(2)}, u32[]{:S(2)}) collective-permute-start(bf16[128,1024]{1,0:T(8,128)(2,1)} %collective-permute-done.11.refs_2_), channel_id=1, source_target_pairs={{0,16},{1,9},{2,18},{3,11},{4,20},{5,13},{6,22},{7,15},{8,24},{9,1... | collective-permute-start | bytes 786440 | tf_op jit(solution)/shard_map/ppermute | solution.py:41
  60.9 6.6 %copy-start.1 = (bf16[144,1024]{1,0:T(8,128)(2,1)S(1)}, bf16[144,1024]{1,0:T(8,128)(2,1)}, u32[]{:S(2)}) copy-start(bf16[144,1024]{1,0:T(8,128)(2,1)} %copy-done) | copy-start | bytes 884740
  60.9 6.6 %copy-start.3 = (bf16[144,1024]{1,0:T(8,128)(2,1)S(1)}, bf16[144,1024]{1,0:T(8,128)(2,1)}, u32[]{:S(2)}) copy-start(bf16[144,1024]{1,0:T(8,128)(2,1)} %copy-done.2) | copy-start | bytes 884740
  60.9 6.6 %copy-start.6 = (bf16[144,1024]{1,0:T(8,128)(2,1)S(1)}, bf16[144,1024]{1,0:T(8,128)(2,1)}, u32[]{:S(2)}) copy-start(bf16[144,1024]{1,0:T(8,128)(2,1)} %copy-done.5) | copy-start | bytes 884740
  60.9 6.6 %copy-start.13 = (bf16[144,1024]{1,0:T(8,128)(2,1)S(1)}, bf16[144,1024]{1,0:T(8,128)(2,1)}, u32[]{:S(2)}) copy-start(bf16[144,1024]{1,0:T(8,128)(2,1)} %copy-done.12) | copy-start | bytes 884740
  60.9 6.7 %copy-start.15 = (bf16[144,1024]{1,0:T(8,128)(2,1)S(1)}, bf16[144,1024]{1,0:T(8,128)(2,1)}, u32[]{:S(2)}) copy-start(bf16[144,1024]{1,0:T(8,128)(2,1)} %copy-done.14) | copy-start | bytes 884740
  61.0 6.7 %copy-start.17 = (bf16[144,1024]{1,0:T(8,128)(2,1)S(1)}, bf16[144,1024]{1,0:T(8,128)(2,1)}, u32[]{:S(2)}) copy-start(bf16[144,1024]{1,0:T(8,128)(2,1)} %copy-done.16) | copy-start | bytes 884740
  61.0 6.8 %copy-start.19 = (bf16[144,1024]{1,0:T(8,128)(2,1)S(1)}, bf16[144,1024]{1,0:T(8,128)(2,1)}, u32[]{:S(2)}) copy-start(bf16[144,1024]{1,0:T(8,128)(2,1)} %copy-done.18) | copy-start | bytes 884740
  67.8 3.5 %copy-start.9 = (bf16[128,1024]{1,0:T(8,128)(2,1)S(1)}, bf16[128,1024]{1,0:T(8,128)(2,1)}, u32[]{:S(2)}) copy-start(bf16[128,1024]{1,0:T(8,128)(2,1)} %copy-done.8) | copy-start | bytes 786436
  67.8 4.1 %copy-start.21 = (bf16[128,1024]{1,0:T(8,128)(2,1)S(1)}, bf16[128,1024]{1,0:T(8,128)(2,1)}, u32[]{:S(2)}) copy-start(bf16[128,1024]{1,0:T(8,128)(2,1)} %copy-done.20) | copy-start | bytes 786436
  71.4 9.6 %collective-permute-start.14 = (bf16[128,1024]{1,0:T(8,128)(2,1)S(1)}, bf16[128,1024]{1,0:T(8,128)(2,1)S(1)}, u32[]{:S(2)}, u32[]{:S(2)}) collective-permute-start(bf16[128,1024]{1,0:T(8,128)(2,1)S(1)} %copy-done.9), channel_id=1, source_target_pairs={{0,1},{1,0},{2,3},{3,2},{4,5},{5,4},{6,7},{7,6},{8,9},{9,8},{10,11... | collective-permute-start | bytes 786440 | tf_op jit(solution)/shard_map/ppermute | solution.py:41
  71.4 9.5 %collective-permute-start.15 = (bf16[128,1024]{1,0:T(8,128)(2,1)}, bf16[128,1024]{1,0:T(8,128)(2,1)S(1)}, u32[]{:S(2)}, u32[]{:S(2)}) collective-permute-start(bf16[128,1024]{1,0:T(8,128)(2,1)} %collective-permute-done.11.refs_2_), channel_id=1, source_target_pairs={{0,1},{1,0},{2,3},{3,2},{4,5},{5,4},{6,7},{7,6},{8,9},{9,8},{10,11... | collective-permute-start | bytes 786440 | tf_op jit(solution)/shard_map/ppermute | solution.py:41
  71.9 9.0 %collective-permute-start.16 = (bf16[128,1024]{1,0:T(8,128)(2,1)S(1)}, bf16[128,1024]{1,0:T(8,128)(2,1)S(1)}, u32[]{:S(2)}, u32[]{:S(2)}) collective-permute-start(bf16[128,1024]{1,0:T(8,128)(2,1)S(1)} %copy-done.21), channel_id=1, source_target_pairs={{0,1},{1,0},{2,3},{3,2},{4,5},{5,4},{6,7},{7,6},{8,9},{9,8},{10,11... | collective-permute-start | bytes 786440 | tf_op jit(solution)/shard_map/ppermute | solution.py:41
  72.0 9.0 %collective-permute-start.17 = (bf16[128,1024]{1,0:T(8,128)(2,1)}, bf16[128,1024]{1,0:T(8,128)(2,1)S(1)}, u32[]{:S(2)}, u32[]{:S(2)}) collective-permute-start(bf16[128,1024]{1,0:T(8,128)(2,1)} %collective-permute-done.13.refs_4_), channel_id=1, source_target_pairs={{0,1},{1,0},{2,3},{3,2},{4,5},{5,4},{6,7},{7,6},{8,9},{9,8},{10,11... | collective-permute-start | bytes 786440 | tf_op jit(solution)/shard_map/ppermute | solution.py:41
  76.7 4.3 %copy-start.4 = (bf16[144,1024]{1,0:T(8,128)(2,1)S(1)}, bf16[144,1024]{1,0:T(8,128)(2,1)}, u32[]{:S(2)}) copy-start(bf16[144,1024]{1,0:T(8,128)(2,1)} %copy-done.2) | copy-start | bytes 884740
  76.7 4.3 %copy-start.7 = (bf16[144,1024]{1,0:T(8,128)(2,1)S(1)}, bf16[144,1024]{1,0:T(8,128)(2,1)}, u32[]{:S(2)}) copy-start(bf16[144,1024]{1,0:T(8,128)(2,1)} %copy-done.5) | copy-start | bytes 884740
  80.9 17.8 %copy-start.24 = (f32[128]{0:T(128)S(1)}, f32[128]{0:T(128)}, u32[]{:S(2)}) copy-start(f32[128]{0:T(128)} %param.10) | copy-start | bytes 1540
  86.2 12.4 %all-to-all-start = ((f32[32,3,128]{2,1,0:T(4,128)}), f32[32,3,128]{2,1,0:T(4,128)S(1)}, u32[]{:S(2)}, u32[]{:S(2)}) async-start(f32[32,3,128]{2,1,0:T(4,128)} %bitcast.14), calls=%async_computation | async-start | bytes 131072 | tf_op jit(solution)/shard_map/all_to_all | solution.py:275
  (6 other events, 4.2 us)
where the time goes:
time: 99.6 us; the launch traced here: 99.3 us
  waiting for transfers between devices  34.3 us (34%)
  starting transfers between devices  31.5 us (32%)
  Pallas kernels  23.7 us (24%)
  local copies, waits for them, and re-layouts  7.5 us (8%)
  between operations  1.61 us (2%)
    ppermute x28, waiting for transfers between devices, permute(): return lax.ppermute(a, ('dp', 'tensor'), perm)  27.6 us
    ppermute x28, starting transfers between devices, permute(): return lax.ppermute(a, ('dp', 'tensor'), perm)  26.5 us
    pallas_call x4, Pallas kernels, layer_product(): pl.pallas_call(functools.partial(layer_kernel, n, place, layer, first, la...  16.6 us
    all_to_all x1, waiting for transfers between devices, body(): parts = lax.all_to_all(spread_stats, ('dp', 'tensor'), 0, 0, tiled=True)  6.74 us
    pallas_call x1, Pallas kernels, loaded(): pl.pallas_call(load_kernel, out_shape=pltpu.VMEM(head.shape, head.dtype),...  6.51 us
    unnamed x50, local copies, waits for them, and re-layouts  6.48 us
    all_to_all x1, starting transfers between devices, body(): parts = lax.all_to_all(spread_stats, ('dp', 'tensor'), 0, 0, tiled=True)  5 us
  transfers between devices with their start and end apart: 29, of which 11 were waited for; matrix products, arithmetic and copies ran while one was open for 0% of the time, Pallas kernels for 19%

commit v1 on v0

--- a/solution.py
+++ b/solution.py
@@ -60,10 +60,11 @@
             got[j, 0] = self.plane(a, self.second, j)
         return got
 
-    def fill(self, got):
+    def fill(self, got, *late):
+        late = (*late, *got.values())
         for j in range(1, self.rows):
             for i in range(1, self.cols):
-                got[j, i] = self.plane(got[0, i], self.second, j)
+                got[j, i] = self.plane(after(got[0, i], *late), self.second, j)
         return [got[s] for s in self.spots]
 
     def owners(self, y, x, c):
@@ -132,12 +133,13 @@
         target = to_column(target).astype(jnp.int32)
         pick = jnp.sum(jnp.where(entry == target, logits, 0.0), axis=1, keepdims=True)
         spot = start_ref[2 + CORES + b]
-        out_ref[spot, 0:1, :] = to_row(top)
-        out_ref[spot, 1:2, :] = to_row(total)
-        out_ref[spot, 2:3, :] = to_row(pick)
-
-
-def layer_product(tok, starts, blocks, layer, place, head, acc, marks, last):
+        for peer in range(out_ref.shape[1]):
+            out_ref[spot, peer, 0:1, :] = to_row(top)
+            out_ref[spot, peer, 1:2, :] = to_row(total)
+            out_ref[spot, peer, 2:3, :] = to_row(pick)
+
+
+def layer_product(tok, peers, starts, blocks, layer, place, head, acc, marks, last):
     n = len(place)
     feat = blocks[0].shape[1]
     vocab = head.shape[1]
@@ -151,7 +153,7 @@
     work = 2 * n * tok * CORES * feat * vocab
     return pl.pallas_call(
         functools.partial(layer_kernel, n, place, layer, first, last),
-        out_shape=jax.ShapeDtypeStruct((n, 3, tok), jnp.float32) if last else logits,
+        out_shape=jax.ShapeDtypeStruct((n, peers, 3, tok), jnp.float32) if last else logits,
         in_specs=[pl.BlockSpec(memory_space=pltpu.SMEM)] + [vmem] * (len(operands) - 1),
         out_specs=vmem,
         scratch_shapes=scratch,
@@ -162,15 +164,24 @@
     )(*operands)
 
 
+def fetch(pairs, sems):
+    copies = [pltpu.make_async_copy(a, b, sems.at[i]) for i, (a, b) in enumerate(pairs)]
+    for copy in copies:
+        copy.start()
+    for copy in copies:
+        copy.wait()
+
+
 def norm_kernel(size, *refs):
     blocks, sums, gains, rest = refs[:size], refs[size : size + 2], refs[size + 2 : 2 * size + 2], refs[2 * size + 2 :]
-    out_ref = rest[-1]
+    out_ref, raw, sems = rest[-3:]
     tok, feat = blocks[0].shape
+    fetch([(blocks[j], raw.at[j]) for j in range(size)], sems)
     scale = to_column(lax.rsqrt((sums[0][...] + sums[1][...]) / D + 1e-06))
     for j in range(size):
-        part = blocks[j][...].astype(jnp.float32) * scale * gains[j][:, :feat]
+        part = raw[j].astype(jnp.float32) * scale * gains[j][:, :feat]
         out_ref[j * tok : (j + 1) * tok, :] = part.astype(jnp.bfloat16)
-    if len(rest) > 1:
+    if len(rest) > 3:
         target = rest[0][...]
         row = lax.broadcasted_iota(jnp.int32, (EXTRA, tok), 0)
         digits = jnp.where(row == 0, target >> 14, jnp.where(row == 1, (target >> 7) & 127, target & 127))
@@ -180,22 +191,42 @@
 
 def normalized(blocks, sums, gains, target=None):
     tok, feat = blocks[0].shape
+    size = len(blocks)
     operands = [*blocks, *sums, *gains] + ([] if target is None else [target])
-    rows = len(blocks) * tok + (0 if target is None else EXTRA)
+    rows = size * tok + (0 if target is None else EXTRA)
+    vmem = pl.BlockSpec(memory_space=pltpu.VMEM)
     return pl.pallas_call(
-        functools.partial(norm_kernel, len(blocks)),
+        functools.partial(norm_kernel, size),
         out_shape=jax.ShapeDtypeStruct((rows, feat), jnp.bfloat16),
-        in_specs=[pl.BlockSpec(memory_space=pltpu.VMEM)] * len(operands),
-        out_specs=pl.BlockSpec(memory_space=pltpu.VMEM),
+        in_specs=[pl.BlockSpec(memory_space=pl.ANY)] * size + [vmem] * (len(operands) - size),
+        out_specs=vmem,
+        scratch_shapes=[pltpu.VMEM((size, tok, feat), jnp.bfloat16), pltpu.SemaphoreType.DMA((size,))],
         compiler_params=pltpu.CompilerParams(vmem_limit_bytes=SMALL_LIMIT),
     )(*operands)
 
 
-def squares_kernel(hidden_ref, gain_ref, out_ref):
-    values = hidden_ref[...].astype(jnp.float32)
+def squares_kernel(hidden_ref, gain_ref, out_ref, raw, gain, sems):
+    fetch([(hidden_ref, raw), (gain_ref, gain)], sems)
+    values = raw[...].astype(jnp.float32)
     feat = values.shape[1]
-    out_ref[:, :feat] = gain_ref[...]
+    out_ref[:, :feat] = gain[...]
     out_ref[:, feat:] = to_row(jnp.sum(values * values, axis=1, keepdims=True))
+
+
+def squares(hidden, gain):
+    tok, feat = hidden.shape
+    return pl.pallas_call(
+        squares_kernel,
+        out_shape=jax.ShapeDtypeStruct((1, feat + tok), jnp.float32),
+        in_specs=[pl.BlockSpec(memory_space=pl.ANY)] * 2,
+        out_specs=pl.BlockSpec(memory_space=pltpu.VMEM),
+        scratch_shapes=[
+            pltpu.VMEM((tok, feat), jnp.bfloat16),
+            pltpu.VMEM((1, feat), jnp.float32),
+            pltpu.SemaphoreType.DMA((2,)),
+        ],
+        compiler_params=pltpu.CompilerParams(vmem_limit_bytes=SMALL_LIMIT),
+    )(hidden, gain)
 
 
 def load_kernel(head_ref, out_ref, sem):
@@ -225,11 +256,7 @@
     groups = [[0]] + [[d, depth - d] for d in range(1, (depth + 1) // 2)] + [[depth // 2]]
     place = [grid.sibling_spot(k) for k in range(n_dp)]
 
-    packed = pl.pallas_call(
-        squares_kernel,
-        out_shape=jax.ShapeDtypeStruct((1, feat + tok), jnp.float32),
-        compiler_params=pltpu.CompilerParams(vmem_limit_bytes=SMALL_LIMIT),
-    )(hidden, norm_gain[None, :])
+    packed = squares(hidden, norm_gain[None, :])
     fine = [grid.along(packed, dz) if dz else packed for dz in range(depth)]
     layers = {0: hidden}
     before = []
@@ -239,7 +266,7 @@
         before = [layers[dz] for dz in group]
 
     own_sum = sum(a[:, feat:] for a in fine)
-    own_sum = after(own_sum, layers[1])
+    own_sum = after(own_sum, *(layers[dz] for dz in groups[1]))
     sums = (own_sum, grid.sibling(own_sum))
 
     vocab_cols = head.shape[1]
@@ -254,25 +281,25 @@
         gains = [fine[dz] for dz in group]
         normed.append(normalized(sources, sums, gains, None if at else targets[None, :]))
         reached.append(grid.reach(normed[-1]))
-    near = loaded(after(head, *reached[0].values(), normed[1]))
+    near = loaded(after(head, normed[1]))
     acc, marks = None, None
     for at, group in enumerate(groups):
         final = at == len(groups) - 1
-        spread = grid.fill(dict(reached[at]))
+        held = [] if final or not at else [layers[dz] for dz in groups[at + 1]]
+        spread = grid.fill(dict(reached[at]), *([acc] if at == 1 else []), *held)
         if marks is None:
             marks = spread
         blocks = spread + [grid.sibling(a) for a in spread]
-        following = [] if final else [*reached[at + 1].values(), *normed[at + 2 : at + 3]]
+        following = [] if final or not at else [*reached[at + 1].values(), *normed[at + 2 : at + 3]]
         for layer, dz in enumerate(group):
             start = (z_me - dz) % depth * (CORES * feat)
             starts = [start] + [(c_me - dc) % CORES * feat for dc in range(CORES)] + [vocab_start] + owners
             if layer == len(group) - 1:
                 blocks[0] = after(blocks[0], *following)
             last = final and layer == len(group) - 1
-            acc = layer_product(tok, jnp.stack(starts), blocks, layer, place, near, acc, marks, last)
-
-    spread_stats = jnp.broadcast_to(acc[:, None], (n_dp, n_t, 3, tok)).reshape(n_dp * n_t, 3, tok)
-    parts = lax.all_to_all(spread_stats, ("dp", "tensor"), 0, 0, tiled=True)
+            acc = layer_product(tok, n_t, jnp.stack(starts), blocks, layer, place, near, acc, marks, last)
+
+    parts = lax.all_to_all(acc.reshape(n_dp * n_t, 3, tok), ("dp", "tensor"), 0, 0, tiled=True)
     top = jnp.max(parts[:, 0], axis=0)
     total = jnp.sum(parts[:, 1] * jnp.exp(parts[:, 0] - top[None, :]), axis=0)
     picked = jnp.sum(parts[:, 2], axis=0)

time: 99.6 us -> 120 us (1.20)
  local copies, waits for them, and re-layouts: 7.5 us -> 21.9 us
  Pallas kernels: 23.7 us -> 28.4 us
  waiting for transfers between devices: 34.3 us -> 35.9 us
    unnamed x50 -> x56, local copies, waits for them, and re-layouts: 6.48 us -> 21.5 us
    pallas_call x4, Pallas kernels: 16.6 us -> 19.7 us  [layer_product(): pl.pallas_call(functools.partial(layer_kernel, n, place, layer, first, la...]
    pallas_call x4, Pallas kernels: 0.63 us -> 2.38 us  [the longest x3 2.2 us: normalized(): pl.pallas_call(functools.partial(norm_kernel, size), out_shape=jax.ShapeD...]
    ppermute x28, waiting for transfers between devices: 27.6 us -> 29.1 us  [permute(): return lax.ppermute(a, ('dp', 'tensor'), perm)]
    ppermute x28, starting transfers between devices: 26.5 us -> 25.2 us  [permute(): return lax.ppermute(a, ('dp', 'tensor'), perm)]
  transfers between devices with their start and end apart: 29 -> 29, of which waited for: 11 -> 8; matrix products, arithmetic and copies ran while one was open for 0% -> 0% of each run, Pallas kernels for 19% -> 19%
where the time goes in v1:
time: 120 us
  waiting for transfers between devices  35.9 us (30%)
  starting transfers between devices  31.4 us (26%)
  Pallas kernels  28.4 us (24%)
  local copies, waits for them, and re-layouts  21.9 us (18%)
  between operations  1.66 us (1%)
    ppermute x28, waiting for transfers between devices, permute(): return lax.ppermute(a, ('dp', 'tensor'), perm)  29.1 us
    ppermute x28, starting transfers between devices, permute(): return lax.ppermute(a, ('dp', 'tensor'), perm)  25.2 us
    unnamed x56, local copies, waits for them, and re-layouts  21.5 us
    pallas_call x4, Pallas kernels, layer_product(): pl.pallas_call(functools.partial(layer_kernel, n, place, layer, first, la...  19.7 us
    all_to_all x1, waiting for transfers between devices, body(): lax.all_to_all(acc.reshape(n_dp * n_t, 3, tok), ('dp', 'tensor'), 0, 0, t...  6.74 us
    pallas_call x1, Pallas kernels, loaded(): pl.pallas_call(load_kernel, out_shape=pltpu.VMEM(head.shape, head.dtype),...  6.38 us
    all_to_all x1, starting transfers between devices, body(): lax.all_to_all(acc.reshape(n_dp * n_t, 3, tok), ('dp', 'tensor'), 0, 0, t...  6.17 us
  transfers between devices with their start and end apart: 29, of which 8 were waited for; matrix products, arithmetic and copies ran while one was open for 0% of the time, Pallas kernels for 19%

profile of v1, /device:TPU:0, one launch (start us, length us, event | category | flops | bytes accessed | tf_op | source)
XLA Modules:
  0.0 119.8 jit_solution(6898092098897554312)
XLA Ops:
  0.6 3.1 %collective-permute-start = (bf16[128,1024]{1,0:T(8,128)(2,1)}, bf16[128,1024]{1,0:T(8,128)(2,1)S(1)}, u32[]{:S(2)}, u32[]{:S(2)}) collective-permute-start(bf16[128,1024]{1,0:T(8,128)(2,1)} %refs_0_.1), channel_id=1, source_target_pairs={{0,2},{1,3},{2,4},{3,5},{4,6},{5,7},{6,0},{7,1},{8,10},{9,11},{10,... | collective-permute-start | bytes 786440 | tf_op jit(solution)/shard_map/ppermute | solution.py:41
  3.7 2.1 %collective-permute-start.1 = (bf16[128,1024]{1,0:T(8,128)(2,1)}, bf16[128,1024]{1,0:T(8,128)(2,1)S(1)}, u32[]{:S(2)}, u32[]{:S(2)}) collective-permute-start(bf16[128,1024]{1,0:T(8,128)(2,1)} %refs_0_.1), channel_id=1, source_target_pairs={{0,6},{1,7},{2,0},{3,1},{4,2},{5,3},{6,4},{7,5},{8,14},{9,15},{10,... | collective-permute-start | bytes 786440 | tf_op jit(solution)/shard_map/ppermute | solution.py:41
  5.8 1.0 copy-done.10
  6.8 0.7 copy-done.20
  7.7 2.5 %collective-permute-start.4 = (f32[1,1152]{1,0:T(1,128)S(1)}, f32[1,1152]{1,0:T(1,128)S(1)}, u32[]{:S(2)}, u32[]{:S(2)}) collective-permute-start(f32[1,1152]{1,0:T(1,128)S(1)} %shard_map.77.refs_3_), channel_id=1, source_target_pairs={{0,4},{1,5},{2,6},{3,7},{4,0},{5,1},{6,2},{7,3},{8,12},{9,13},{10,... | collective-permute-start | bytes 13832 | tf_op jit(solution)/shard_map/ppermute | solution.py:41
  10.2 1.3 %collective-permute-start.5 = (f32[1,1152]{1,0:T(1,128)S(1)}, f32[1,1152]{1,0:T(1,128)S(1)}, u32[]{:S(2)}, u32[]{:S(2)}) collective-permute-start(f32[1,1152]{1,0:T(1,128)S(1)} %shard_map.77.refs_3_), channel_id=1, source_target_pairs={{0,6},{1,7},{2,0},{3,1},{4,2},{5,3},{6,4},{7,5},{8,14},{9,15},{10,... | collective-permute-start | bytes 13832 | tf_op jit(solution)/shard_map/ppermute | solution.py:41
  11.6 6.6 %collective-permute-done.3.refs_4_ = f32[1,1152]{1,0:T(1,128)S(1)} collective-permute-done((f32[1,1152]{1,0:T(1,128)S(1)}, f32[1,1152]{1,0:T(1,128)S(1)}, u32[]{:S(2)}, u32[]{:S(2)}) %collective-permute-start.3) | collective-permute-done | bytes 4640 | tf_op jit(solution)/shard_map/ppermute | solution.py:41
  18.3 1.1 collective-permute-done.6.refs_2_.refs_3_
  19.4 0.9 copy-done.11
  20.4 0.7 copy-done.21
  21.2 1.6 %collective-permute-start.7 = (bf16[144,1024]{1,0:T(8,128)(2,1)S(1)}, bf16[144,1024]{1,0:T(8,128)(2,1)S(1)}, u32[]{:S(2)}, u32[]{:S(2)}) collective-permute-start(bf16[144,1024]{1,0:T(8,128)(2,1)S(1)} %shard_map.78.refs_1_.refs_11_), channel_id=1, source_target_pairs={{0,8},{1,17},{2,10},{3,19},{4,12},{5,21},{6,14},{7,23},{8,0},{9,25... | collective-permute-start | bytes 884744 | tf_op jit(solution)/shard_map/ppermute | solution.py:41
  22.8 1.5 %collective-permute-start.8 = (bf16[144,1024]{1,0:T(8,128)(2,1)S(1)}, bf16[144,1024]{1,0:T(8,128)(2,1)S(1)}, u32[]{:S(2)}, u32[]{:S(2)}) collective-permute-start(bf16[144,1024]{1,0:T(8,128)(2,1)S(1)} %shard_map.78.refs_1_.refs_11_), channel_id=1, source_target_pairs={{0,16},{1,9},{2,18},{3,11},{4,20},{5,13},{6,22},{7,15},{8,24},{9,1... | collective-permute-start | bytes 884744 | tf_op jit(solution)/shard_map/ppermute | solution.py:41
  24.3 6.5 %collective-permute-done.7.refs_2_.refs_12_ = bf16[144,1024]{1,0:T(8,128)(2,1)S(1)} collective-permute-done((bf16[144,1024]{1,0:T(8,128)(2,1)S(1)}, bf16[144,1024]{1,0:T(8,128)(2,1)S(1)}, u32[]{:S(2)}, u32[]{:S(2)}) %collective-permute-start.7) | collective-permute-done | bytes 294944 | tf_op jit(solution)/shard_map/ppermute | solution.py:41
  30.8 1.4 %collective-permute-start.18 = (bf16[144,1024]{1,0:T(8,128)(2,1)S(1)}, bf16[144,1024]{1,0:T(8,128)(2,1)S(1)}, u32[]{:S(2)}, u32[]{:S(2)}) collective-permute-start(bf16[144,1024]{1,0:T(8,128)(2,1)S(1)} %collective-permute-done.7.refs_2_.refs_12_), channel_id=1, source_target_pairs={{0,16},{1,9},{2,18},{3,11},{4,20},{5,13},{6,22},{7,15},{8,24},{9,1... | collective-permute-start | bytes 884744 | tf_op jit(solution)/shard_map/ppermute | solution.py:41
  32.2 0.2 shard_map.79.refs_1_
  32.4 0.9 collective-permute-start.10
  33.3 1.2 %collective-permute-start.9 = (bf16[256,1024]{1,0:T(8,128)(2,1)S(1)}, bf16[256,1024]{1,0:T(8,128)(2,1)}, u32[]{:S(2)}, u32[]{:S(2)}) collective-permute-start(bf16[256,1024]{1,0:T(8,128)(2,1)S(1)} %shard_map.79.refs_1_), channel_id=1, source_target_pairs={{0,8},{1,17},{2,10},{3,19},{4,12},{5,21},{6,14},{7,23},{8,0},{9,25... | collective-permute-start | bytes 1572872 | tf_op jit(solution)/shard_map/ppermute | solution.py:41
  34.6 3.5 %collective-permute-done.18.refs_4_.refs_14_ = bf16[144,1024]{1,0:T(8,128)(2,1)S(1)} collective-permute-done((bf16[144,1024]{1,0:T(8,128)(2,1)S(1)}, bf16[144,1024]{1,0:T(8,128)(2,1)S(1)}, u32[]{:S(2)}, u32[]{:S(2)}) %collective-permute-start.18) | collective-permute-done | bytes 294944 | tf_op jit(solution)/shard_map/ppermute | solution.py:41
  38.1 0.8 collective-permute-start.2
  39.0 6.4 %shard_map.81.refs_9_ = bf16[8192,1152]{1,0:T(8,128)(2,1)S(1)} custom-call(bf16[8192,1152]{1,0:T(8,128)(2,1)} %head_ref), custom_call_target="tpu_custom_call" | custom-call | tf_op jit(solution)/shard_map/pallas_call | solution.py:239
  45.5 0.8 copy-done.16
  46.2 1.2 %copy-done.18 = bf16[144,1024]{1,0:T(8,128)(2,1)} copy-done((bf16[144,1024]{1,0:T(8,128)(2,1)}, bf16[144,1024]{1,0:T(8,128)(2,1)S(1)}, u32[]{:S(2)}) %copy-start.18) | copy-done | bytes 294936
  47.4 1.2 copy-done.5
  48.6 1.2 copy-done.8
  49.8 1.2 copy-done.13
  51.0 1.2 copy-done.15
  52.2 1.1 copy-done.17
  53.3 1.0 copy-done.19
  54.2 3.6 %shard_map.82.refs_10_ = f32[512,1152]{1,0:T(8,128)S(1)} custom-call(s32[8]{0:T(128)S(1)} %stack.78.refs_0_, bf16[144,1024]{1,0:T(8,128)(2,1)S(1)} %shard_map.78.refs_1_.refs_11_, bf16[144,1024]{1,0:T(8,128)(2,1)S(1)} %collective-permute-done.7.refs_2_.refs_12_, bf16[144,1024]{1,0:T(8,128)(2,1)S(1)} %copy-done.5, bf16[144,1024]{1,0:T(8,128)(2,1)S(1)} %copy-done.8, ...), custom_call_target="tpu_custom_call" | custom-call | flops 2415919104 | bytes 4718592 | tf_op jit(solution)/shard_map/pallas_call | solution.py:154
  57.8 2.2 %collective-permute-start.23 = (bf16[256,1024]{1,0:T(8,128)(2,1)}, bf16[256,1024]{1,0:T(8,128)(2,1)}, u32[]{:S(2)}, u32[]{:S(2)}) collective-permute-start(bf16[256,1024]{1,0:T(8,128)(2,1)} %collective-permute-done.9.refs_2_), channel_id=1, source_target_pairs={{0,16},{1,9},{2,18},{3,11},{4,20},{5,13},{6,22},{7,15},{8,24},{9,1... | collective-permute-start | bytes 1572872 | tf_op jit(solution)/shard_map/ppermute | solution.py:41
  60.1 1.8 %shard_map.80.refs_1_ = bf16[128,1024]{1,0:T(8,128)(2,1)} custom-call(bf16[128,1024]{1,0:T(8,128)(2,1)} %collective-permute-done.2.refs_0_, f32[1,128]{1,0:T(1,128)S(1)} %slice_add_fusion.refs_1_.refs_2_, f32[1,128]{1,0:T(1,128)S(1)} %collective-permute-done.6.refs_2_.refs_3_, f32[1,1152]{1,0:T(1,128)S(1)} %collective-permute-done.4.refs_3_), custom_call_target="tpu_custom_call" | custom-call | tf_op jit(solution)/shard_map/pallas_call | solution.py:198
  61.9 2.6 %collective-permute-start.11 = (bf16[128,1024]{1,0:T(8,128)(2,1)}, bf16[128,1024]{1,0:T(8,128)(2,1)}, u32[]{:S(2)}, u32[]{:S(2)}) collective-permute-start(bf16[128,1024]{1,0:T(8,128)(2,1)} %shard_map.80.refs_1_), channel_id=1, source_target_pairs={{0,8},{1,17},{2,10},{3,19},{4,12},{5,21},{6,14},{7,23},{8,0},{9,25... | collective-permute-start | bytes 786440 | tf_op jit(solution)/shard_map/ppermute | solution.py:41
  64.5 0.5 collective-permute-start.25
  65.0 7.0 %collective-permute-done.11.refs_2_ = bf16[128,1024]{1,0:T(8,128)(2,1)} collective-permute-done((bf16[128,1024]{1,0:T(8,128)(2,1)}, bf16[128,1024]{1,0:T(8,128)(2,1)}, u32[]{:S(2)}, u32[]{:S(2)}) %collective-permute-start.11) | collective-permute-done | bytes 262176 | tf_op jit(solution)/shard_map/ppermute | solution.py:41
  72.1 0.5 collective-permute-start.27
  72.6 0.6 collective-permute-done.12.refs_3_
  73.2 2.0 %collective-permute-start.13 = (bf16[128,1024]{1,0:T(8,128)(2,1)}, bf16[128,1024]{1,0:T(8,128)(2,1)}, u32[]{:S(2)}, u32[]{:S(2)}) collective-permute-start(bf16[128,1024]{1,0:T(8,128)(2,1)} %collective-permute-done.11.refs_2_), channel_id=1, source_target_pairs={{0,16},{1,9},{2,18},{3,11},{4,20},{5,13},{6,22},{7,15},{8,24},{9,1... | collective-permute-start | bytes 786440 | tf_op jit(solution)/shard_map/ppermute | solution.py:41
  75.5 0.5 collective-permute-start.15
  76.1 3.7 %collective-permute-done.13.refs_4_ = bf16[128,1024]{1,0:T(8,128)(2,1)} collective-permute-done((bf16[128,1024]{1,0:T(8,128)(2,1)}, bf16[128,1024]{1,0:T(8,128)(2,1)}, u32[]{:S(2)}, u32[]{:S(2)}) %collective-permute-start.13) | collective-permute-done | bytes 262176 | tf_op jit(solution)/shard_map/ppermute | solution.py:41
  79.9 6.4 %copy-done.1 = bf16[8192,1152]{1,0:T(8,128)(2,1)S(1)} copy-done((bf16[8192,1152]{1,0:T(8,128)(2,1)S(1)}, bf16[8192,1152]{1,0:T(8,128)(2,1)}, u32[]{:S(2)}) %copy-start.1) | copy-done | bytes 18874392
  86.2 5.1 %shard_map.83.refs_10_ = f32[512,1152]{1,0:T(8,128)S(1)} custom-call(s32[8]{0:T(128)S(1)} %stack.80.refs_0_, bf16[256,1024]{1,0:T(8,128)(2,1)S(1)} %shard_map.79.refs_1_, bf16[256,1024]{1,0:T(8,128)(2,1)} %collective-permute-done.9.refs_2_, bf16[256,1024]{1,0:T(8,128)(2,1)} %collective-permute-done.10.refs_3_, ...), custom_call_target="tpu_custom_call" | custom-call | flops 2415919104 | bytes 4718592 | tf_op jit(solution)/shard_map/pallas_call | solution.py:154
  91.4 1.4 %copy-done.2 = f32[512,1152]{1,0:T(8,128)} copy-done((f32[512,1152]{1,0:T(8,128)}, f32[512,1152]{1,0:T(8,128)S(1)}, u32[]{:S(2)}) %copy-start.2) | copy-done | bytes 2359320
  92.8 1.7 %copy-done.3 = f32[512,1152]{1,0:T(8,128)S(1)} copy-done((f32[512,1152]{1,0:T(8,128)S(1)}, f32[512,1152]{1,0:T(8,128)}, u32[]{:S(2)}) %copy-start.3) | copy-done | bytes 2359320
  94.5 5.1 %shard_map.84.refs_10_ = f32[512,1152]{1,0:T(8,128)S(1)} custom-call(s32[8]{0:T(128)S(1)} %stack.76.refs_0_, bf16[256,1024]{1,0:T(8,128)(2,1)S(1)} %shard_map.79.refs_1_, bf16[256,1024]{1,0:T(8,128)(2,1)} %collective-permute-done.9.refs_2_, bf16[256,1024]{1,0:T(8,128)(2,1)} %collective-permute-done.10.refs_3_, ...), custom_call_target="tpu_custom_call" | custom-call | flops 2415919104 | bytes 4718592 | tf_op jit(solution)/shard_map/pallas_call | solution.py:154
  99.8 5.8 %shard_map.85 = f32[4,8,3,128]{3,2,1,0:T(4,128)} custom-call(s32[8]{0:T(128)S(1)} %stack.74.refs_0_, bf16[128,1024]{1,0:T(8,128)(2,1)} %shard_map.80.refs_1_, bf16[128,1024]{1,0:T(8,128)(2,1)} %collective-permute-done.11.refs_2_, bf16[128,1024]{1,0:T(8,128)(2,1)} %collective-permute-done.12.refs_3_, bf16[128,1024]{1,0:T(8,128)(2,1)} %collective-permute-done.13.refs_4_, ...), custom_call_target="tpu_custom_call" | custom-call | flops 2415919104 | bytes 4718592 | tf_op jit(solution)/shard_map/pallas_call | solution.py:154
  105.6 6.2 %all-to-all-start = ((f32[32,3,128]{2,1,0:T(4,128)}), f32[32,3,128]{2,1,0:T(4,128)S(1)}, u32[]{:S(2)}, u32[]{:S(2)}) async-start(f32[32,3,128]{2,1,0:T(4,128)} %bitcast.14), calls=%async_computation | async-start | bytes 131072 | tf_op jit(solution)/shard_map/all_to_all | solution.py:302
  112.4 6.7 %all-to-all-done = f32[32,3,128]{2,1,0:T(4,128)S(1)} async-done(((f32[32,3,128]{2,1,0:T(4,128)}), f32[32,3,128]{2,1,0:T(4,128)S(1)}, u32[]{:S(2)}, u32[]{:S(2)}) %all-to-all-start) | async-done | bytes 49184 | tf_op jit(solution)/shard_map/all_to_all | solution.py:302
  119.2 0.5 compare_select_fusion
  (85 shorter events, 1.3 us)
Async XLA Ops:
  0.6 17.6 %collective-permute-start = (bf16[128,1024]{1,0:T(8,128)(2,1)}, bf16[128,1024]{1,0:T(8,128)(2,1)S(1)}, u32[]{:S(2)}, u32[]{:S(2)}) collective-permute-start(bf16[128,1024]{1,0:T(8,128)(2,1)} %refs_0_.1), channel_id=1, source_target_pairs={{0,2},{1,3},{2,4},{3,5},{4,6},{5,7},{6,0},{7,1},{8,10},{9,11},{10,... | collective-permute-start | bytes 786440 | tf_op jit(solution)/shard_map/ppermute | solution.py:41
  3.7 14.5 %collective-permute-start.1 = (bf16[128,1024]{1,0:T(8,128)(2,1)}, bf16[128,1024]{1,0:T(8,128)(2,1)S(1)}, u32[]{:S(2)}, u32[]{:S(2)}) collective-permute-start(bf16[128,1024]{1,0:T(8,128)(2,1)} %refs_0_.1), channel_id=1, source_target_pairs={{0,6},{1,7},{2,0},{3,1},{4,2},{5,3},{6,4},{7,5},{8,14},{9,15},{10,... | collective-permute-start | bytes 786440 | tf_op jit(solution)/shard_map/ppermute | solution.py:41
  7.7 10.5 %collective-permute-start.3 = (f32[1,1152]{1,0:T(1,128)S(1)}, f32[1,1152]{1,0:T(1,128)S(1)}, u32[]{:S(2)}, u32[]{:S(2)}) collective-permute-start(f32[1,1152]{1,0:T(1,128)S(1)} %shard_map.77.refs_3_), channel_id=1, source_target_pairs={{0,2},{1,3},{2,4},{3,5},{4,6},{5,7},{6,0},{7,1},{8,10},{9,11},{10,... | collective-permute-start | bytes 13832 | tf_op jit(solution)/shard_map/ppermute | solution.py:41
  7.7 10.5 %collective-permute-start.4 = (f32[1,1152]{1,0:T(1,128)S(1)}, f32[1,1152]{1,0:T(1,128)S(1)}, u32[]{:S(2)}, u32[]{:S(2)}) collective-permute-start(f32[1,1152]{1,0:T(1,128)S(1)} %shard_map.77.refs_3_), channel_id=1, source_target_pairs={{0,4},{1,5},{2,6},{3,7},{4,0},{5,1},{6,2},{7,3},{8,12},{9,13},{10,... | collective-permute-start | bytes 13832 | tf_op jit(solution)/shard_map/ppermute | solution.py:41
  10.2 8.0 %collective-permute-start.5 = (f32[1,1152]{1,0:T(1,128)S(1)}, f32[1,1152]{1,0:T(1,128)S(1)}, u32[]{:S(2)}, u32[]{:S(2)}) collective-permute-start(f32[1,1152]{1,0:T(1,128)S(1)} %shard_map.77.refs_3_), channel_id=1, source_target_pairs={{0,6},{1,7},{2,0},{3,1},{4,2},{5,3},{6,4},{7,5},{8,14},{9,15},{10,... | collective-permute-start | bytes 13832 | tf_op jit(solution)/shard_map/ppermute | solution.py:41
  18.2 1.2 collective-permute-start.6
  21.2 9.5 %collective-permute-start.7 = (bf16[144,1024]{1,0:T(8,128)(2,1)S(1)}, bf16[144,1024]{1,0:T(8,128)(2,1)S(1)}, u32[]{:S(2)}, u32[]{:S(2)}) collective-permute-start(bf16[144,1024]{1,0:T(8,128)(2,1)S(1)} %shard_map.78.refs_1_.refs_11_), channel_id=1, source_target_pairs={{0,8},{1,17},{2,10},{3,19},{4,12},{5,21},{6,14},{7,23},{8,0},{9,25... | collective-permute-start | bytes 884744 | tf_op jit(solution)/shard_map/ppermute | solution.py:41
  22.8 8.0 %collective-permute-start.8 = (bf16[144,1024]{1,0:T(8,128)(2,1)S(1)}, bf16[144,1024]{1,0:T(8,128)(2,1)S(1)}, u32[]{:S(2)}, u32[]{:S(2)}) collective-permute-start(bf16[144,1024]{1,0:T(8,128)(2,1)S(1)} %shard_map.78.refs_1_.refs_11_), channel_id=1, source_target_pairs={{0,16},{1,9},{2,18},{3,11},{4,20},{5,13},{6,22},{7,15},{8,24},{9,1... | collective-permute-start | bytes 884744 | tf_op jit(solution)/shard_map/ppermute | solution.py:41
  24.3 10.3 %collective-permute-start.19 = (bf16[144,1024]{1,0:T(8,128)(2,1)S(1)}, bf16[144,1024]{1,0:T(8,128)(2,1)S(1)}, u32[]{:S(2)}, u32[]{:S(2)}) collective-permute-start(bf16[144,1024]{1,0:T(8,128)(2,1)S(1)} %shard_map.78.refs_1_.refs_11_), channel_id=1, source_target_pairs={{0,1},{1,0},{2,3},{3,2},{4,5},{5,4},{6,7},{7,6},{8,9},{9,8},{10,11... | collective-permute-start | bytes 884744 | tf_op jit(solution)/shard_map/ppermute | solution.py:41
  30.8 14.6 %copy-start.4 = (bf16[144,1024]{1,0:T(8,128)(2,1)}, bf16[144,1024]{1,0:T(8,128)(2,1)S(1)}, u32[]{:S(2)}) copy-start(bf16[144,1024]{1,0:T(8,128)(2,1)S(1)} %collective-permute-done.8.refs_3_.refs_13_) | copy-start | bytes 884740
  30.8 7.3 %collective-permute-start.18 = (bf16[144,1024]{1,0:T(8,128)(2,1)S(1)}, bf16[144,1024]{1,0:T(8,128)(2,1)S(1)}, u32[]{:S(2)}, u32[]{:S(2)}) collective-permute-start(bf16[144,1024]{1,0:T(8,128)(2,1)S(1)} %collective-permute-done.7.refs_2_.refs_12_), channel_id=1, source_target_pairs={{0,16},{1,9},{2,18},{3,11},{4,20},{5,13},{6,22},{7,15},{8,24},{9,1... | collective-permute-start | bytes 884744 | tf_op jit(solution)/shard_map/ppermute | solution.py:41
  32.2 6.0 %collective-permute-start.20 = (bf16[144,1024]{1,0:T(8,128)(2,1)S(1)}, bf16[144,1024]{1,0:T(8,128)(2,1)S(1)}, u32[]{:S(2)}, u32[]{:S(2)}) collective-permute-start(bf16[144,1024]{1,0:T(8,128)(2,1)S(1)} %collective-permute-done.7.refs_2_.refs_12_), channel_id=1, source_target_pairs={{0,1},{1,0},{2,3},{3,2},{4,5},{5,4},{6,7},{7,6},{8,9},{9,8},{10,11... | collective-permute-start | bytes 884744 | tf_op jit(solution)/shard_map/ppermute | solution.py:41
  32.4 25.4 %collective-permute-start.10 = (bf16[256,1024]{1,0:T(8,128)(2,1)S(1)}, bf16[256,1024]{1,0:T(8,128)(2,1)}, u32[]{:S(2)}, u32[]{:S(2)}) collective-permute-start(bf16[256,1024]{1,0:T(8,128)(2,1)S(1)} %shard_map.79.refs_1_), channel_id=1, source_target_pairs={{0,16},{1,9},{2,18},{3,11},{4,20},{5,13},{6,22},{7,15},{8,24},{9,1... | collective-permute-start | bytes 1572872 | tf_op jit(solution)/shard_map/ppermute | solution.py:41
  33.3 24.5 %collective-permute-start.9 = (bf16[256,1024]{1,0:T(8,128)(2,1)S(1)}, bf16[256,1024]{1,0:T(8,128)(2,1)}, u32[]{:S(2)}, u32[]{:S(2)}) collective-permute-start(bf16[256,1024]{1,0:T(8,128)(2,1)S(1)} %shard_map.79.refs_1_), channel_id=1, source_target_pairs={{0,8},{1,17},{2,10},{3,19},{4,12},{5,21},{6,14},{7,23},{8,0},{9,25... | collective-permute-start | bytes 1572872 | tf_op jit(solution)/shard_map/ppermute | solution.py:41
  34.6 10.8 %copy-start.12 = (bf16[144,1024]{1,0:T(8,128)(2,1)}, bf16[144,1024]{1,0:T(8,128)(2,1)S(1)}, u32[]{:S(2)}) copy-start(bf16[144,1024]{1,0:T(8,128)(2,1)S(1)} %collective-permute-done.19.refs_5_) | copy-start | bytes 884740
  34.6 10.9 %collective-permute-start.21 = (bf16[144,1024]{1,0:T(8,128)(2,1)S(1)}, bf16[144,1024]{1,0:T(8,128)(2,1)S(1)}, u32[]{:S(2)}, u32[]{:S(2)}) collective-permute-start(bf16[144,1024]{1,0:T(8,128)(2,1)S(1)} %collective-permute-done.8.refs_3_.refs_13_), channel_id=1, source_target_pairs={{0,1},{1,0},{2,3},{3,2},{4,5},{5,4},{6,7},{7,6},{8,9},{9,8},{10,11... | collective-permute-start | bytes 884744 | tf_op jit(solution)/shard_map/ppermute | solution.py:41
  38.1 7.3 %copy-start.7 = (bf16[144,1024]{1,0:T(8,128)(2,1)}, bf16[144,1024]{1,0:T(8,128)(2,1)S(1)}, u32[]{:S(2)}) copy-start(bf16[144,1024]{1,0:T(8,128)(2,1)S(1)} %collective-permute-done.18.refs_4_.refs_14_) | copy-start | bytes 884740
  38.1 8.1 %collective-permute-start.22 = (bf16[144,1024]{1,0:T(8,128)(2,1)S(1)}, bf16[144,1024]{1,0:T(8,128)(2,1)S(1)}, u32[]{:S(2)}, u32[]{:S(2)}) collective-permute-start(bf16[144,1024]{1,0:T(8,128)(2,1)S(1)} %collective-permute-done.18.refs_4_.refs_14_), channel_id=1, source_target_pairs={{0,1},{1,0},{2,3},{3,2},{4,5},{5,4},{6,7},{7,6},{8,9},{9,8},{10,11... | collective-permute-start | bytes 884744 | tf_op jit(solution)/shard_map/ppermute | solution.py:41
  38.1 7.3 %copy-start.14 = (bf16[144,1024]{1,0:T(8,128)(2,1)}, bf16[144,1024]{1,0:T(8,128)(2,1)S(1)}, u32[]{:S(2)}) copy-start(bf16[144,1024]{1,0:T(8,128)(2,1)S(1)} %collective-permute-done.20.refs_6_) | copy-start | bytes 884740
  38.1 19.7 %collective-permute-start.2 = (bf16[128,1024]{1,0:T(8,128)(2,1)}, bf16[128,1024]{1,0:T(8,128)(2,1)}, u32[]{:S(2)}, u32[]{:S(2)}) collective-permute-start(bf16[128,1024]{1,0:T(8,128)(2,1)} %refs_0_.1), channel_id=1, source_target_pairs={{0,4},{1,5},{2,6},{3,7},{4,0},{5,1},{6,2},{7,3},{8,12},{9,13},{10,... | collective-permute-start | bytes 786440 | tf_op jit(solution)/shard_map/ppermute | solution.py:41
  45.4 12.4 %copy-start = (bf16[8192,1152]{1,0:T(8,128)(2,1)}, bf16[8192,1152]{1,0:T(8,128)(2,1)S(1)}, u32[]{:S(2)}) copy-start(bf16[8192,1152]{1,0:T(8,128)(2,1)S(1)} %shard_map.81.refs_9_) | copy-start | bytes 56623108
  46.2 1.2 %copy-start.18 = (bf16[144,1024]{1,0:T(8,128)(2,1)}, bf16[144,1024]{1,0:T(8,128)(2,1)S(1)}, u32[]{:S(2)}) copy-start(bf16[144,1024]{1,0:T(8,128)(2,1)S(1)} %collective-permute-done.22.refs_8_) | copy-start | bytes 884740
  48.6 1.2 copy-start.8
  49.8 1.2 copy-start.13
  57.8 14.2 %collective-permute-start.23 = (bf16[256,1024]{1,0:T(8,128)(2,1)}, bf16[256,1024]{1,0:T(8,128)(2,1)}, u32[]{:S(2)}, u32[]{:S(2)}) collective-permute-start(bf16[256,1024]{1,0:T(8,128)(2,1)} %collective-permute-done.9.refs_2_), channel_id=1, source_target_pairs={{0,16},{1,9},{2,18},{3,11},{4,20},{5,13},{6,22},{7,15},{8,24},{9,1... | collective-permute-start | bytes 1572872 | tf_op jit(solution)/shard_map/ppermute | solution.py:41
  61.9 10.2 %collective-permute-start.11 = (bf16[128,1024]{1,0:T(8,128)(2,1)}, bf16[128,1024]{1,0:T(8,128)(2,1)}, u32[]{:S(2)}, u32[]{:S(2)}) collective-permute-start(bf16[128,1024]{1,0:T(8,128)(2,1)} %shard_map.80.refs_1_), channel_id=1, source_target_pairs={{0,8},{1,17},{2,10},{3,19},{4,12},{5,21},{6,14},{7,23},{8,0},{9,25... | collective-permute-start | bytes 786440 | tf_op jit(solution)/shard_map/ppermute | solution.py:41
  64.5 10.9 %collective-permute-start.24 = (bf16[256,1024]{1,0:T(8,128)(2,1)S(1)}, bf16[256,1024]{1,0:T(8,128)(2,1)}, u32[]{:S(2)}, u32[]{:S(2)}) collective-permute-start(bf16[256,1024]{1,0:T(8,128)(2,1)S(1)} %shard_map.79.refs_1_), channel_id=1, source_target_pairs={{0,1},{1,0},{2,3},{3,2},{4,5},{5,4},{6,7},{7,6},{8,9},{9,8},{10,11... | collective-permute-start | bytes 1572872 | tf_op jit(solution)/shard_map/ppermute | solution.py:41
  64.5 8.7 %collective-permute-start.12 = (bf16[128,1024]{1,0:T(8,128)(2,1)}, bf16[128,1024]{1,0:T(8,128)(2,1)}, u32[]{:S(2)}, u32[]{:S(2)}) collective-permute-start(bf16[128,1024]{1,0:T(8,128)(2,1)} %shard_map.80.refs_1_), channel_id=1, source_target_pairs={{0,16},{1,9},{2,18},{3,11},{4,20},{5,13},{6,22},{7,15},{8,24},{9,1... | collective-permute-start | bytes 786440 | tf_op jit(solution)/shard_map/ppermute | solution.py:41
  64.5 11.0 %collective-permute-start.25 = (bf16[256,1024]{1,0:T(8,128)(2,1)}, bf16[256,1024]{1,0:T(8,128)(2,1)}, u32[]{:S(2)}, u32[]{:S(2)}) collective-permute-start(bf16[256,1024]{1,0:T(8,128)(2,1)} %collective-permute-done.9.refs_2_), channel_id=1, source_target_pairs={{0,1},{1,0},{2,3},{3,2},{4,5},{5,4},{6,7},{7,6},{8,9},{9,8},{10,11... | collective-permute-start | bytes 1572872 | tf_op jit(solution)/shard_map/ppermute | solution.py:41
  72.0 4.0 %collective-permute-start.26 = (bf16[256,1024]{1,0:T(8,128)(2,1)}, bf16[256,1024]{1,0:T(8,128)(2,1)}, u32[]{:S(2)}, u32[]{:S(2)}) collective-permute-start(bf16[256,1024]{1,0:T(8,128)(2,1)} %collective-permute-done.10.refs_3_), channel_id=1, source_target_pairs={{0,1},{1,0},{2,3},{3,2},{4,5},{5,4},{6,7},{7,6},{8,9},{9,8},{10,11... | collective-permute-start | bytes 1572872 | tf_op jit(solution)/shard_map/ppermute | solution.py:41
  72.1 7.8 %collective-permute-start.27 = (bf16[256,1024]{1,0:T(8,128)(2,1)}, bf16[256,1024]{1,0:T(8,128)(2,1)}, u32[]{:S(2)}, u32[]{:S(2)}) collective-permute-start(bf16[256,1024]{1,0:T(8,128)(2,1)} %collective-permute-done.23.refs_4_), channel_id=1, source_target_pairs={{0,1},{1,0},{2,3},{3,2},{4,5},{5,4},{6,7},{7,6},{8,9},{9,8},{10,11... | collective-permute-start | bytes 1572872 | tf_op jit(solution)/shard_map/ppermute | solution.py:41
  73.2 6.7 %collective-permute-start.13 = (bf16[128,1024]{1,0:T(8,128)(2,1)}, bf16[128,1024]{1,0:T(8,128)(2,1)}, u32[]{:S(2)}, u32[]{:S(2)}) collective-permute-start(bf16[128,1024]{1,0:T(8,128)(2,1)} %collective-permute-done.11.refs_2_), channel_id=1, source_target_pairs={{0,16},{1,9},{2,18},{3,11},{4,20},{5,13},{6,22},{7,15},{8,24},{9,1... | collective-permute-start | bytes 786440 | tf_op jit(solution)/shard_map/ppermute | solution.py:41
  75.5 24.2 %collective-permute-start.14 = (bf16[128,1024]{1,0:T(8,128)(2,1)}, bf16[128,1024]{1,0:T(8,128)(2,1)}, u32[]{:S(2)}, u32[]{:S(2)}) collective-permute-start(bf16[128,1024]{1,0:T(8,128)(2,1)} %shard_map.80.refs_1_), channel_id=1, source_target_pairs={{0,1},{1,0},{2,3},{3,2},{4,5},{5,4},{6,7},{7,6},{8,9},{9,8},{10,11... | collective-permute-start | bytes 786440 | tf_op jit(solution)/shard_map/ppermute | solution.py:41
  75.5 24.1 %collective-permute-start.15 = (bf16[128,1024]{1,0:T(8,128)(2,1)}, bf16[128,1024]{1,0:T(8,128)(2,1)}, u32[]{:S(2)}, u32[]{:S(2)}) collective-permute-start(bf16[128,1024]{1,0:T(8,128)(2,1)} %collective-permute-done.11.refs_2_), channel_id=1, source_target_pairs={{0,1},{1,0},{2,3},{3,2},{4,5},{5,4},{6,7},{7,6},{8,9},{9,8},{10,11... | collective-permute-start | bytes 786440 | tf_op jit(solution)/shard_map/ppermute | solution.py:41
  76.0 23.6 %collective-permute-start.16 = (bf16[128,1024]{1,0:T(8,128)(2,1)}, bf16[128,1024]{1,0:T(8,128)(2,1)}, u32[]{:S(2)}, u32[]{:S(2)}) collective-permute-start(bf16[128,1024]{1,0:T(8,128)(2,1)} %collective-permute-done.12.refs_3_), channel_id=1, source_target_pairs={{0,1},{1,0},{2,3},{3,2},{4,5},{5,4},{6,7},{7,6},{8,9},{9,8},{10,11... | collective-permute-start | bytes 786440 | tf_op jit(solution)/shard_map/ppermute | solution.py:41
  79.9 19.8 %collective-permute-start.17 = (bf16[128,1024]{1,0:T(8,128)(2,1)}, bf16[128,1024]{1,0:T(8,128)(2,1)}, u32[]{:S(2)}, u32[]{:S(2)}) collective-permute-start(bf16[128,1024]{1,0:T(8,128)(2,1)} %collective-permute-done.13.refs_4_), channel_id=1, source_target_pairs={{0,1},{1,0},{2,3},{3,2},{4,5},{5,4},{6,7},{7,6},{8,9},{9,8},{10,11... | collective-permute-start | bytes 786440 | tf_op jit(solution)/shard_map/ppermute | solution.py:41
  79.9 6.4 %copy-start.1 = (bf16[8192,1152]{1,0:T(8,128)(2,1)S(1)}, bf16[8192,1152]{1,0:T(8,128)(2,1)}, u32[]{:S(2)}) copy-start(bf16[8192,1152]{1,0:T(8,128)(2,1)} %copy-done) | copy-start | bytes 56623108
  86.2 13.5 %slice-start = ((s8[18874368]{0:T(1024)(128)(4,1)}), s8[4194304]{0:T(1024)(128)(4,1)S(1)}, s32[]{:S(2)}) async-start(s8[18874368]{0:T(1024)(128)(4,1)} %bitcast.20), calls=%async_computation.1 | async-start | bytes 8388608
  86.2 13.5 %slice-start.1 = ((s8[18874368]{0:T(1024)(128)(4,1)}), s8[4194304]{0:T(1024)(128)(4,1)S(1)}, s32[]{:S(2)}) async-start(s8[18874368]{0:T(1024)(128)(4,1)} %bitcast.20), calls=%async_computation.2 | async-start | bytes 8388608
  86.2 13.5 %slice-start.2 = ((s8[18874368]{0:T(1024)(128)(4,1)}), s8[4194304]{0:T(1024)(128)(4,1)S(1)}, s32[]{:S(2)}) async-start(s8[18874368]{0:T(1024)(128)(4,1)} %bitcast.20), calls=%async_computation.3 | async-start | bytes 8388608
  91.4 1.4 %copy-start.2 = (f32[512,1152]{1,0:T(8,128)}, f32[512,1152]{1,0:T(8,128)S(1)}, u32[]{:S(2)}) copy-start(f32[512,1152]{1,0:T(8,128)S(1)} %shard_map.83.refs_10_) | copy-start | bytes 7077892
  92.8 1.7 %copy-start.3 = (f32[512,1152]{1,0:T(8,128)S(1)}, f32[512,1152]{1,0:T(8,128)}, u32[]{:S(2)}) copy-start(f32[512,1152]{1,0:T(8,128)} %copy-done.2) | copy-start | bytes 7077892
  94.5 5.2 %slice-start.3 = ((s8[18874368]{0:T(1024)(128)(4,1)}), s8[4194304]{0:T(1024)(128)(4,1)S(1)}, s32[]{:S(2)}) async-start(s8[18874368]{0:T(1024)(128)(4,1)} %bitcast.20), calls=%async_computation.4 | async-start | bytes 8388608
  94.5 5.3 %slice-start.4 = ((s8[18874368]{0:T(1024)(128)(4,1)}), s8[2097152]{0:T(1024)(128)(4,1)S(1)}, s32[]{:S(2)}) async-start(s8[18874368]{0:T(1024)(128)(4,1)} %bitcast.20), calls=%async_computation.5 | async-start | bytes 4194304
  94.5 5.3 %copy-start.6 = (bf16[144,1024]{1,0:T(8,128)(2,1)S(1)}, bf16[144,1024]{1,0:T(8,128)(2,1)}, u32[]{:S(2)}) copy-start(bf16[144,1024]{1,0:T(8,128)(2,1)} %copy-done.4) | copy-start | bytes 884740
  94.5 5.3 %copy-start.9 = (bf16[144,1024]{1,0:T(8,128)(2,1)S(1)}, bf16[144,1024]{1,0:T(8,128)(2,1)}, u32[]{:S(2)}) copy-start(bf16[144,1024]{1,0:T(8,128)(2,1)} %copy-done.7) | copy-start | bytes 884740
  99.6 19.6 %copy-start.22 = (f32[128]{0:T(128)S(1)}, f32[128]{0:T(128)}, u32[]{:S(2)}) copy-start(f32[128]{0:T(128)} %param.10) | copy-start | bytes 1540
  105.6 13.6 %all-to-all-start = ((f32[32,3,128]{2,1,0:T(4,128)}), f32[32,3,128]{2,1,0:T(4,128)S(1)}, u32[]{:S(2)}, u32[]{:S(2)}) async-start(f32[32,3,128]{2,1,0:T(4,128)} %bitcast.14), calls=%async_computation | async-start | bytes 131072 | tf_op jit(solution)/shard_map/all_to_all | solution.py:302
  (9 other events, 8.5 us)

commit v2 on v1

--- a/solution.py
+++ b/solution.py
@@ -10,8 +10,7 @@
 D = 8192
 CORES = 2
 X_ONLY, Y_ONLY = (0, 1), (1, 0)
-VMEM_LIMIT = 16 * 1024 * 1024
-LOAD_LIMIT = 36 * 1024 * 1024
+VMEM_LIMIT = 20 * 1024 * 1024
 SMALL_LIMIT = 6 * 1024 * 1024
 EXTRA = 16
 BASE = 128
@@ -83,6 +82,10 @@
         return self.spots.index((i, j)) if self.square else k
 
 
+def far(a):
+    return pltpu.with_memory_space_constraint(a, pltpu.HBM)
+
+
 def after(a, *others):
     return lax.optimization_barrier((a, *others))[0] if others else a
 
@@ -107,19 +110,30 @@
     head_ref = refs.pop(0)
     acc_ref = None if first else refs.pop(0)
     marks = [refs.pop(0) for _ in range(n)] if last else None
-    out_ref, rows, acc = refs if last else (*refs, refs[0])
+    out_ref, rows, weights, sems = refs[:4]
+    acc = refs[4] if last else out_ref
     tok = rows.shape[0] // n
     feat = blocks[0].shape[1]
+    copies = []
+    for half in range(CORES):
+        offset = pl.multiple_of(start_ref[0] + half * feat, feat)
+        source = head_ref.at[pl.ds(offset, feat)]
+        copies.append(pltpu.make_async_copy(source, weights.at[half], sems.at[half]))
+        copies[-1].start()
     for c in range(CORES):
         columns = pl.ds(pl.multiple_of(start_ref[1 + c], feat), feat)
         for k in range(n):
             spot = place[k] if c else k
             part = blocks[c * n + k][layer * tok : (layer + 1) * tok, :]
             rows[spot * tok : (spot + 1) * tok, columns] = part
-    offset = pl.multiple_of(start_ref[0], CORES * feat)
-    weights = head_ref[pl.ds(offset, CORES * feat), :]
-    product = jnp.dot(rows[...], weights, preferred_element_type=jnp.float32)
-    acc[...] = product if first else acc_ref[...] + product
+    for half in range(CORES):
+        copies[half].wait()
+        part = rows[:, half * feat : (half + 1) * feat]
+        product = jnp.dot(part, weights[half], preferred_element_type=jnp.float32)
+        if half:
+            acc[...] += product
+        else:
+            acc[...] = product if first else acc_ref[...] + product
     if not last:
         return
     base = start_ref[1 + CORES]
@@ -146,15 +160,22 @@
     vmem = pl.BlockSpec(memory_space=pltpu.VMEM)
     first = acc is None
     logits = jax.ShapeDtypeStruct((n * tok, vocab), jnp.float32)
-    operands = [starts, *blocks, head] + ([] if first else [acc]) + (marks if last else [])
-    scratch = [pltpu.VMEM((n * tok, CORES * feat), jnp.bfloat16)]
+    operands = [starts, *blocks, far(head)] + ([] if first else [acc]) + (marks if last else [])
+    specs = [vmem] * len(operands)
+    specs[0] = pl.BlockSpec(memory_space=pltpu.SMEM)
+    specs[1 + len(blocks)] = pl.BlockSpec(memory_space=pltpu.HBM)
+    scratch = [
+        pltpu.VMEM((n * tok, CORES * feat), jnp.bfloat16),
+        pltpu.VMEM((CORES, feat, vocab), jnp.bfloat16),
+        pltpu.SemaphoreType.DMA((CORES,)),
+    ]
     if last:
         scratch.append(pltpu.VMEM(logits.shape, jnp.float32))
     work = 2 * n * tok * CORES * feat * vocab
     return pl.pallas_call(
         functools.partial(layer_kernel, n, place, layer, first, last),
         out_shape=jax.ShapeDtypeStruct((n, peers, 3, tok), jnp.float32) if last else logits,
-        in_specs=[pl.BlockSpec(memory_space=pltpu.SMEM)] + [vmem] * (len(operands) - 1),
+        in_specs=specs,
         out_specs=vmem,
         scratch_shapes=scratch,
         compiler_params=pltpu.CompilerParams(vmem_limit_bytes=VMEM_LIMIT),
@@ -174,15 +195,20 @@
 
 def norm_kernel(size, *refs):
     blocks, sums, gains, rest = refs[:size], refs[size : size + 2], refs[size + 2 : 2 * size + 2], refs[2 * size + 2 :]
-    out_ref, raw, sems = rest[-3:]
+    out_ref, raw, sems = rest[1], rest[2], rest[-1]
+    if len(rest) == 3:
+        out_ref, raw = rest[0], rest[1]
     tok, feat = blocks[0].shape
-    fetch([(blocks[j], raw.at[j]) for j in range(size)], sems)
+    with_target = len(rest) > 3
+    target = rest[3] if with_target else None
+    pairs = [(blocks[j], raw.at[j]) for j in range(size)] + ([(rest[0], target)] if with_target else [])
+    fetch(pairs, sems)
     scale = to_column(lax.rsqrt((sums[0][...] + sums[1][...]) / D + 1e-06))
     for j in range(size):
         part = raw[j].astype(jnp.float32) * scale * gains[j][:, :feat]
         out_ref[j * tok : (j + 1) * tok, :] = part.astype(jnp.bfloat16)
-    if len(rest) > 3:
-        target = rest[0][...]
+    if with_target:
+        target = target[...]
         row = lax.broadcasted_iota(jnp.int32, (EXTRA, tok), 0)
         digits = jnp.where(row == 0, target >> 14, jnp.where(row == 1, (target >> 7) & 127, target & 127))
         out_ref[tok:, :] = jnp.zeros((EXTRA, feat), jnp.bfloat16)
@@ -192,15 +218,22 @@
 def normalized(blocks, sums, gains, target=None):
     tok, feat = blocks[0].shape
     size = len(blocks)
-    operands = [*blocks, *sums, *gains] + ([] if target is None else [target])
+    if target is not None:
+        blocks = [far(a) for a in blocks]
+    operands = [*blocks, *sums, *gains] + ([] if target is None else [far(target)])
     rows = size * tok + (0 if target is None else EXTRA)
-    vmem = pl.BlockSpec(memory_space=pltpu.VMEM)
+    vmem, whole = pl.BlockSpec(memory_space=pltpu.VMEM), pl.BlockSpec(memory_space=pl.ANY)
+    specs = [whole] * size + [vmem] * (len(sums) + size) + ([] if target is None else [whole])
+    scratch = [pltpu.VMEM((size, tok, feat), jnp.bfloat16)]
+    if target is not None:
+        scratch.append(pltpu.VMEM(target.shape, target.dtype))
+    scratch.append(pltpu.SemaphoreType.DMA((size + 1,)))
     return pl.pallas_call(
         functools.partial(norm_kernel, size),
         out_shape=jax.ShapeDtypeStruct((rows, feat), jnp.bfloat16),
-        in_specs=[pl.BlockSpec(memory_space=pl.ANY)] * size + [vmem] * (len(operands) - size),
+        in_specs=specs,
         out_specs=vmem,
-        scratch_shapes=[pltpu.VMEM((size, tok, feat), jnp.bfloat16), pltpu.SemaphoreType.DMA((size,))],
+        scratch_shapes=scratch,
         compiler_params=pltpu.CompilerParams(vmem_limit_bytes=SMALL_LIMIT),
     )(*operands)
 
@@ -226,24 +259,7 @@
             pltpu.SemaphoreType.DMA((2,)),
         ],
         compiler_params=pltpu.CompilerParams(vmem_limit_bytes=SMALL_LIMIT),
-    )(hidden, gain)
-
-
-def load_kernel(head_ref, out_ref, sem):
-    copy = pltpu.make_async_copy(head_ref, out_ref, sem)
-    copy.start()
-    copy.wait()
-
-
-def loaded(head):
-    return pl.pallas_call(
-        load_kernel,
-        out_shape=pltpu.VMEM(head.shape, head.dtype),
-        in_specs=[pl.BlockSpec(memory_space=pl.ANY)],
-        out_specs=pl.BlockSpec(memory_space=pltpu.VMEM),
-        scratch_shapes=[pltpu.SemaphoreType.DMA],
-        compiler_params=pltpu.CompilerParams(vmem_limit_bytes=LOAD_LIMIT),
-    )(head)
+    )(far(hidden), far(gain))
 
 
 def body(hidden, norm_gain, head, targets, old_logprob, lengths):
@@ -277,15 +293,15 @@
     for at, group in enumerate(groups):
         sources = [layers[dz] for dz in group]
         if at:
-            sources[0] = after(sources[0], *reached[-1].values())
+            earlier = [normed[0]] if at == 1 else list(reached[-1].values())
+            sources[0] = after(sources[0], *earlier)
         gains = [fine[dz] for dz in group]
         normed.append(normalized(sources, sums, gains, None if at else targets[None, :]))
         reached.append(grid.reach(normed[-1]))
-    near = loaded(after(head, normed[1]))
     acc, marks = None, None
     for at, group in enumerate(groups):
         final = at == len(groups) - 1
-        held = [] if final or not at else [layers[dz] for dz in groups[at + 1]]
+        held = [] if final else [layers[dz] for dz in groups[at + 1]] if at else [normed[1]]
         spread = grid.fill(dict(reached[at]), *([acc] if at == 1 else []), *held)
         if marks is None:
             marks = spread
@@ -297,7 +313,7 @@
             if layer == len(group) - 1:
                 blocks[0] = after(blocks[0], *following)
             last = final and layer == len(group) - 1
-            acc = layer_product(tok, n_t, jnp.stack(starts), blocks, layer, place, near, acc, marks, last)
+            acc = layer_product(tok, n_t, jnp.stack(starts), blocks, layer, place, head, acc, marks, last)
 
     parts = lax.all_to_all(acc.reshape(n_dp * n_t, 3, tok), ("dp", "tensor"), 0, 0, tiled=True)
     top = jnp.max(parts[:, 0], axis=0)

time: 120 us -> 114 us (0.950)
  local copies, waits for them, and re-layouts: 21.9 us -> 10.4 us
  waiting for transfers between devices: 35.9 us -> 40 us
  Pallas kernels: 28.4 us -> 32.2 us
  starting transfers between devices: 31.4 us -> 28.7 us
    unnamed x56 -> x30, local copies, waits for them, and re-layouts: 21.5 us -> 10.1 us
    pallas_call x4, Pallas kernels: 19.7 us -> 27.9 us  [layer_product(): pl.pallas_call(functools.partial(layer_kernel, n, place, layer, first, la...]
    pallas_call x1 -> x0, Pallas kernels: 6.38 us -> none  [loaded(): pl.pallas_call(load_kernel, out_shape=pltpu.VMEM(head.shape, head.dtype),...]
    ppermute x28, waiting for transfers between devices: 29.1 us -> 33.2 us  [permute(): return lax.ppermute(a, ('dp', 'tensor'), perm)]
    all_to_all x1, starting transfers between devices: 6.17 us -> 4.5 us  [body(): lax.all_to_all(acc.reshape(n_dp * n_t, 3, tok), ('dp', 'tensor'), 0, 0, t...]
  transfers between devices with their start and end apart: 29 -> 29, of which waited for: 8 -> 8; matrix products, arithmetic and copies ran while one was open for 0% -> 0% of each run, Pallas kernels for 19% -> 21%
where the time goes in v2:
time: 114 us; the launch traced here: 113 us
  waiting for transfers between devices  40 us (35%)
  Pallas kernels  32.2 us (28%)
  starting transfers between devices  28.7 us (25%)
  local copies, waits for them, and re-layouts  10.4 us (9%)
  between operations  1.54 us (1%)
    ppermute x28, waiting for transfers between devices, permute(): return lax.ppermute(a, ('dp', 'tensor'), perm)  33.2 us
    pallas_call x4, Pallas kernels, layer_product(): pl.pallas_call(functools.partial(layer_kernel, n, place, layer, first, la...  27.9 us
    ppermute x28, starting transfers between devices, permute(): return lax.ppermute(a, ('dp', 'tensor'), perm)  24.2 us
    unnamed x30, local copies, waits for them, and re-layouts  10.1 us
    all_to_all x1, waiting for transfers between devices, body(): lax.all_to_all(acc.reshape(n_dp * n_t, 3, tok), ('dp', 'tensor'), 0, 0, t...  6.74 us
    all_to_all x1, starting transfers between devices, body(): lax.all_to_all(acc.reshape(n_dp * n_t, 3, tok), ('dp', 'tensor'), 0, 0, t...  4.5 us
    pallas_call x3, Pallas kernels, normalized(): pl.pallas_call(functools.partial(norm_kernel, size), out_shape=jax.ShapeD...  3.16 us
  transfers between devices with their start and end apart: 29, of which 8 were waited for; matrix products, arithmetic and copies ran while one was open for 0% of the time, Pallas kernels for 21%

profile of v2, /device:TPU:0, one launch (start us, length us, event | category | flops | bytes accessed | tf_op | source)
XLA Modules:
  0.0 113.4 jit_solution(6449578419997876023)
XLA Ops:
  0.6 3.1 %collective-permute-start = (bf16[128,1024]{1,0:T(8,128)(2,1)}, bf16[128,1024]{1,0:T(8,128)(2,1)S(1)}, u32[]{:S(2)}, u32[]{:S(2)}) collective-permute-start(bf16[128,1024]{1,0:T(8,128)(2,1)} %refs_0_.1), channel_id=1, source_target_pairs={{0,2},{1,3},{2,4},{3,5},{4,6},{5,7},{6,0},{7,1},{8,10},{9,11},{10,... | collective-permute-start | bytes 786440 | tf_op jit(solution)/shard_map/ppermute | solution.py:40
  3.7 2.1 %collective-permute-start.1 = (bf16[128,1024]{1,0:T(8,128)(2,1)}, bf16[128,1024]{1,0:T(8,128)(2,1)S(1)}, u32[]{:S(2)}, u32[]{:S(2)}) collective-permute-start(bf16[128,1024]{1,0:T(8,128)(2,1)} %refs_0_.1), channel_id=1, source_target_pairs={{0,6},{1,7},{2,0},{3,1},{4,2},{5,3},{6,4},{7,5},{8,14},{9,15},{10,... | collective-permute-start | bytes 786440 | tf_op jit(solution)/shard_map/ppermute | solution.py:40
  5.8 1.1 %shard_map.77.refs_3_ = f32[1,1152]{1,0:T(1,128)S(1)} custom-call(bf16[128,1024]{1,0:T(8,128)(2,1)} %refs_0_.1, f32[1,1024]{1,0:T(1,128)} %bitcast.23), custom_call_target="tpu_custom_call" | custom-call | tf_op jit(solution)/shard_map/pallas_call | solution.py:251
  7.0 2.5 %collective-permute-start.4 = (f32[1,1152]{1,0:T(1,128)S(1)}, f32[1,1152]{1,0:T(1,128)S(1)}, u32[]{:S(2)}, u32[]{:S(2)}) collective-permute-start(f32[1,1152]{1,0:T(1,128)S(1)} %shard_map.77.refs_3_), channel_id=1, source_target_pairs={{0,4},{1,5},{2,6},{3,7},{4,0},{5,1},{6,2},{7,3},{8,12},{9,13},{10,... | collective-permute-start | bytes 13832 | tf_op jit(solution)/shard_map/ppermute | solution.py:40
  9.5 1.3 %collective-permute-start.5 = (f32[1,1152]{1,0:T(1,128)S(1)}, f32[1,1152]{1,0:T(1,128)S(1)}, u32[]{:S(2)}, u32[]{:S(2)}) collective-permute-start(f32[1,1152]{1,0:T(1,128)S(1)} %shard_map.77.refs_3_), channel_id=1, source_target_pairs={{0,6},{1,7},{2,0},{3,1},{4,2},{5,3},{6,4},{7,5},{8,14},{9,15},{10,... | collective-permute-start | bytes 13832 | tf_op jit(solution)/shard_map/ppermute | solution.py:40
  10.9 7.3 %collective-permute-done.3.refs_4_ = f32[1,1152]{1,0:T(1,128)S(1)} collective-permute-done((f32[1,1152]{1,0:T(1,128)S(1)}, f32[1,1152]{1,0:T(1,128)S(1)}, u32[]{:S(2)}, u32[]{:S(2)}) %collective-permute-start.3) | collective-permute-done | bytes 4640 | tf_op jit(solution)/shard_map/ppermute | solution.py:40
  18.3 1.1 collective-permute-done.6.refs_2_.refs_3_
  19.4 1.1 shard_map.78.refs_1_.refs_11_
  20.5 1.6 %collective-permute-start.16 = (bf16[144,1024]{1,0:T(8,128)(2,1)S(1)}, bf16[144,1024]{1,0:T(8,128)(2,1)S(1)}, u32[]{:S(2)}, u32[]{:S(2)}) collective-permute-start(bf16[144,1024]{1,0:T(8,128)(2,1)S(1)} %shard_map.78.refs_1_.refs_11_), channel_id=1, source_target_pairs={{0,8},{1,17},{2,10},{3,19},{4,12},{5,21},{6,14},{7,23},{8,0},{9,25... | collective-permute-start | bytes 884744 | tf_op jit(solution)/shard_map/ppermute | solution.py:40
  22.1 1.5 %collective-permute-start.17 = (bf16[144,1024]{1,0:T(8,128)(2,1)S(1)}, bf16[144,1024]{1,0:T(8,128)(2,1)S(1)}, u32[]{:S(2)}, u32[]{:S(2)}) collective-permute-start(bf16[144,1024]{1,0:T(8,128)(2,1)S(1)} %shard_map.78.refs_1_.refs_11_), channel_id=1, source_target_pairs={{0,16},{1,9},{2,18},{3,11},{4,20},{5,13},{6,22},{7,15},{8,24},{9,1... | collective-permute-start | bytes 884744 | tf_op jit(solution)/shard_map/ppermute | solution.py:40
  23.6 0.2 shard_map.79.refs_1_
  23.9 6.2 %collective-permute-done.16.refs_2_.refs_12_ = bf16[144,1024]{1,0:T(8,128)(2,1)S(1)} collective-permute-done((bf16[144,1024]{1,0:T(8,128)(2,1)S(1)}, bf16[144,1024]{1,0:T(8,128)(2,1)S(1)}, u32[]{:S(2)}, u32[]{:S(2)}) %collective-permute-start.16) | collective-permute-done | bytes 294944 | tf_op jit(solution)/shard_map/ppermute | solution.py:40
  30.1 1.4 %collective-permute-start.18 = (bf16[144,1024]{1,0:T(8,128)(2,1)S(1)}, bf16[144,1024]{1,0:T(8,128)(2,1)S(1)}, u32[]{:S(2)}, u32[]{:S(2)}) collective-permute-start(bf16[144,1024]{1,0:T(8,128)(2,1)S(1)} %collective-permute-done.16.refs_2_.refs_12_), channel_id=1, source_target_pairs={{0,16},{1,9},{2,18},{3,11},{4,20},{5,13},{6,22},{7,15},{8,24},{9,1... | collective-permute-start | bytes 884744 | tf_op jit(solution)/shard_map/ppermute | solution.py:40
  31.5 1.5 %collective-permute-start.7 = (bf16[256,1024]{1,0:T(8,128)(2,1)S(1)}, bf16[256,1024]{1,0:T(8,128)(2,1)}, u32[]{:S(2)}, u32[]{:S(2)}) collective-permute-start(bf16[256,1024]{1,0:T(8,128)(2,1)S(1)} %shard_map.79.refs_1_), channel_id=1, source_target_pairs={{0,8},{1,17},{2,10},{3,19},{4,12},{5,21},{6,14},{7,23},{8,0},{9,25... | collective-permute-start | bytes 1572872 | tf_op jit(solution)/shard_map/ppermute | solution.py:40
  33.0 0.6 collective-permute-start.8
  33.6 0.7 copy-done.6
  34.3 0.7 copy-done
  35.0 4.0 %collective-permute-done.18.refs_4_.refs_14_ = bf16[144,1024]{1,0:T(8,128)(2,1)S(1)} collective-permute-done((bf16[144,1024]{1,0:T(8,128)(2,1)S(1)}, bf16[144,1024]{1,0:T(8,128)(2,1)S(1)}, u32[]{:S(2)}, u32[]{:S(2)}) %collective-permute-start.18) | collective-permute-done | bytes 294944 | tf_op jit(solution)/shard_map/ppermute | solution.py:40
  39.0 0.7 copy-done.3
  39.8 0.7 copy-done.8
  40.5 0.7 collective-permute-start.2
  41.3 0.7 copy-done.10
  42.0 0.7 copy-done.12
  42.8 1.0 copy-done.1
  43.7 1.0 copy-done.4
  44.7 1.0 copy-done.7
  45.6 1.0 copy-done.9
  46.6 1.0 copy-done.11
  47.6 1.0 copy-done.13
  48.5 5.7 %shard_map.81.refs_10_ = f32[512,1152]{1,0:T(8,128)S(1)} custom-call(s32[8]{0:T(128)S(1)} %stack.78.refs_0_, bf16[144,1024]{1,0:T(8,128)(2,1)S(1)} %shard_map.78.refs_1_.refs_11_, bf16[144,1024]{1,0:T(8,128)(2,1)S(1)} %collective-permute-done.16.refs_2_.refs_12_, bf16[144,1024]{1,0:T(8,128)(2,1)S(1)} %copy-done.1, bf16[144,1024]{1,0:T(8,128)(2,1)S(1)} %copy-done.4, ...), custom_call_target="tpu_custom_call" | custom-call | flops 2415919104 | bytes 4718592 | tf_op jit(solution)/shard_map/pallas_call | solution.py:175
  54.2 1.8 %collective-permute-done.2.refs_0_ = bf16[128,1024]{1,0:T(8,128)(2,1)} collective-permute-done((bf16[128,1024]{1,0:T(8,128)(2,1)}, bf16[128,1024]{1,0:T(8,128)(2,1)}, u32[]{:S(2)}, u32[]{:S(2)}) %collective-permute-start.2) | collective-permute-done | bytes 262176 | tf_op jit(solution)/shard_map/ppermute | solution.py:40
  56.1 2.2 %collective-permute-start.23 = (bf16[256,1024]{1,0:T(8,128)(2,1)}, bf16[256,1024]{1,0:T(8,128)(2,1)}, u32[]{:S(2)}, u32[]{:S(2)}) collective-permute-start(bf16[256,1024]{1,0:T(8,128)(2,1)} %collective-permute-done.7.refs_2_), channel_id=1, source_target_pairs={{0,16},{1,9},{2,18},{3,11},{4,20},{5,13},{6,22},{7,15},{8,24},{9,1... | collective-permute-start | bytes 1572872 | tf_op jit(solution)/shard_map/ppermute | solution.py:40
  58.2 1.8 %shard_map.80.refs_1_ = bf16[128,1024]{1,0:T(8,128)(2,1)} custom-call(bf16[128,1024]{1,0:T(8,128)(2,1)} %collective-permute-done.2.refs_0_, f32[1,128]{1,0:T(1,128)S(1)} %slice_add_fusion.refs_1_.refs_2_, f32[1,128]{1,0:T(1,128)S(1)} %collective-permute-done.6.refs_2_.refs_3_, f32[1,1152]{1,0:T(1,128)S(1)} %collective-permute-done.4.refs_3_), custom_call_target="tpu_custom_call" | custom-call | tf_op jit(solution)/shard_map/pallas_call | solution.py:231
  60.2 1.6 %collective-permute-start.9 = (bf16[128,1024]{1,0:T(8,128)(2,1)}, bf16[128,1024]{1,0:T(8,128)(2,1)}, u32[]{:S(2)}, u32[]{:S(2)}) collective-permute-start(bf16[128,1024]{1,0:T(8,128)(2,1)} %shard_map.80.refs_1_), channel_id=1, source_target_pairs={{0,8},{1,17},{2,10},{3,19},{4,12},{5,21},{6,14},{7,23},{8,0},{9,25... | collective-permute-start | bytes 786440 | tf_op jit(solution)/shard_map/ppermute | solution.py:40
  61.8 0.6 collective-permute-start.25
  62.4 9.0 %collective-permute-done.10.refs_3_ = bf16[128,1024]{1,0:T(8,128)(2,1)} collective-permute-done((bf16[128,1024]{1,0:T(8,128)(2,1)}, bf16[128,1024]{1,0:T(8,128)(2,1)}, u32[]{:S(2)}, u32[]{:S(2)}) %collective-permute-start.10) | collective-permute-done | bytes 262176 | tf_op jit(solution)/shard_map/ppermute | solution.py:40
  71.3 0.5 collective-permute-start.27
  71.8 2.0 %collective-permute-start.11 = (bf16[128,1024]{1,0:T(8,128)(2,1)}, bf16[128,1024]{1,0:T(8,128)(2,1)}, u32[]{:S(2)}, u32[]{:S(2)}) collective-permute-start(bf16[128,1024]{1,0:T(8,128)(2,1)} %collective-permute-done.9.refs_2_), channel_id=1, source_target_pairs={{0,16},{1,9},{2,18},{3,11},{4,20},{5,13},{6,22},{7,15},{8,24},{9,1... | collective-permute-start | bytes 786440 | tf_op jit(solution)/shard_map/ppermute | solution.py:40
  73.9 0.1 stack.80.refs_0_
  74.2 0.5 collective-permute-start.13
  74.7 0.1 collective-permute-start.14
  74.8 3.7 %collective-permute-done.11.refs_4_ = bf16[128,1024]{1,0:T(8,128)(2,1)} collective-permute-done((bf16[128,1024]{1,0:T(8,128)(2,1)}, bf16[128,1024]{1,0:T(8,128)(2,1)}, u32[]{:S(2)}, u32[]{:S(2)}) %collective-permute-start.11) | collective-permute-done | bytes 262176 | tf_op jit(solution)/shard_map/ppermute | solution.py:40
  78.5 7.2 %shard_map.82.refs_10_ = f32[512,1152]{1,0:T(8,128)S(1)} custom-call(s32[8]{0:T(128)S(1)} %stack.80.refs_0_, bf16[256,1024]{1,0:T(8,128)(2,1)S(1)} %shard_map.79.refs_1_, bf16[256,1024]{1,0:T(8,128)(2,1)} %collective-permute-done.7.refs_2_, bf16[256,1024]{1,0:T(8,128)(2,1)} %collective-permute-done.8.refs_3_, ...), custom_call_target="tpu_custom_call" | custom-call | flops 2415919104 | bytes 4718592 | tf_op jit(solution)/shard_map/pallas_call | solution.py:175
  85.8 7.3 %shard_map.83.refs_10_ = f32[512,1152]{1,0:T(8,128)S(1)} custom-call(s32[8]{0:T(128)S(1)} %stack.76.refs_0_, bf16[256,1024]{1,0:T(8,128)(2,1)S(1)} %shard_map.79.refs_1_, bf16[256,1024]{1,0:T(8,128)(2,1)} %collective-permute-done.7.refs_2_, bf16[256,1024]{1,0:T(8,128)(2,1)} %collective-permute-done.8.refs_3_, ...), custom_call_target="tpu_custom_call" | custom-call | flops 2415919104 | bytes 4718592 | tf_op jit(solution)/shard_map/pallas_call | solution.py:175
  93.2 7.7 %shard_map.84 = f32[4,8,3,128]{3,2,1,0:T(4,128)} custom-call(s32[8]{0:T(128)S(1)} %stack.74.refs_0_, bf16[128,1024]{1,0:T(8,128)(2,1)} %shard_map.80.refs_1_, bf16[128,1024]{1,0:T(8,128)(2,1)} %collective-permute-done.9.refs_2_, bf16[128,1024]{1,0:T(8,128)(2,1)} %collective-permute-done.10.refs_3_, bf16[128,1024]{1,0:T(8,128)(2,1)} %collective-permute-done.11.refs_4_, ...), custom_call_target="tpu_custom_call" | custom-call | flops 2415919104 | bytes 4718592 | tf_op jit(solution)/shard_map/pallas_call | solution.py:175
  100.9 4.5 %all-to-all-start = ((f32[32,3,128]{2,1,0:T(4,128)}), f32[32,3,128]{2,1,0:T(4,128)S(1)}, u32[]{:S(2)}, u32[]{:S(2)}) async-start(f32[32,3,128]{2,1,0:T(4,128)} %bitcast.14), calls=%async_computation | async-start | bytes 131072 | tf_op jit(solution)/shard_map/all_to_all | solution.py:318
  106.0 6.7 %all-to-all-done = f32[32,3,128]{2,1,0:T(4,128)S(1)} async-done(((f32[32,3,128]{2,1,0:T(4,128)}), f32[32,3,128]{2,1,0:T(4,128)S(1)}, u32[]{:S(2)}, u32[]{:S(2)}) %all-to-all-start) | async-done | bytes 49184 | tf_op jit(solution)/shard_map/all_to_all | solution.py:318
  112.9 0.5 compare_select_fusion
  (57 shorter events, 0.8 us)
Async XLA Ops:
  0.6 17.6 %collective-permute-start = (bf16[128,1024]{1,0:T(8,128)(2,1)}, bf16[128,1024]{1,0:T(8,128)(2,1)S(1)}, u32[]{:S(2)}, u32[]{:S(2)}) collective-permute-start(bf16[128,1024]{1,0:T(8,128)(2,1)} %refs_0_.1), channel_id=1, source_target_pairs={{0,2},{1,3},{2,4},{3,5},{4,6},{5,7},{6,0},{7,1},{8,10},{9,11},{10,... | collective-permute-start | bytes 786440 | tf_op jit(solution)/shard_map/ppermute | solution.py:40
  3.7 14.5 %collective-permute-start.1 = (bf16[128,1024]{1,0:T(8,128)(2,1)}, bf16[128,1024]{1,0:T(8,128)(2,1)S(1)}, u32[]{:S(2)}, u32[]{:S(2)}) collective-permute-start(bf16[128,1024]{1,0:T(8,128)(2,1)} %refs_0_.1), channel_id=1, source_target_pairs={{0,6},{1,7},{2,0},{3,1},{4,2},{5,3},{6,4},{7,5},{8,14},{9,15},{10,... | collective-permute-start | bytes 786440 | tf_op jit(solution)/shard_map/ppermute | solution.py:40
  6.9 11.3 %collective-permute-start.3 = (f32[1,1152]{1,0:T(1,128)S(1)}, f32[1,1152]{1,0:T(1,128)S(1)}, u32[]{:S(2)}, u32[]{:S(2)}) collective-permute-start(f32[1,1152]{1,0:T(1,128)S(1)} %shard_map.77.refs_3_), channel_id=1, source_target_pairs={{0,2},{1,3},{2,4},{3,5},{4,6},{5,7},{6,0},{7,1},{8,10},{9,11},{10,... | collective-permute-start | bytes 13832 | tf_op jit(solution)/shard_map/ppermute | solution.py:40
  7.0 11.2 %collective-permute-start.4 = (f32[1,1152]{1,0:T(1,128)S(1)}, f32[1,1152]{1,0:T(1,128)S(1)}, u32[]{:S(2)}, u32[]{:S(2)}) collective-permute-start(f32[1,1152]{1,0:T(1,128)S(1)} %shard_map.77.refs_3_), channel_id=1, source_target_pairs={{0,4},{1,5},{2,6},{3,7},{4,0},{5,1},{6,2},{7,3},{8,12},{9,13},{10,... | collective-permute-start | bytes 13832 | tf_op jit(solution)/shard_map/ppermute | solution.py:40
  9.5 8.7 %collective-permute-start.5 = (f32[1,1152]{1,0:T(1,128)S(1)}, f32[1,1152]{1,0:T(1,128)S(1)}, u32[]{:S(2)}, u32[]{:S(2)}) collective-permute-start(f32[1,1152]{1,0:T(1,128)S(1)} %shard_map.77.refs_3_), channel_id=1, source_target_pairs={{0,6},{1,7},{2,0},{3,1},{4,2},{5,3},{6,4},{7,5},{8,14},{9,15},{10,... | collective-permute-start | bytes 13832 | tf_op jit(solution)/shard_map/ppermute | solution.py:40
  18.2 1.2 %collective-permute-start.6 = (f32[1,128]{1,0:T(1,128)S(1)}, f32[1,128]{1,0:T(1,128)S(1)}, u32[]{:S(2)}, u32[]{:S(2)}) collective-permute-start(f32[1,128]{1,0:T(1,128)S(1)} %slice_add_fusion.refs_1_.refs_2_), channel_id=1, source_target_pairs={{0,1},{1,0},{2,3},{3,2},{4,5},{5,4},{6,7},{7,6},{8,9},{9,8},{10,11... | collective-permute-start | bytes 1544 | tf_op jit(solution)/shard_map/ppermute | solution.py:40
  20.5 9.5 %collective-permute-start.16 = (bf16[144,1024]{1,0:T(8,128)(2,1)S(1)}, bf16[144,1024]{1,0:T(8,128)(2,1)S(1)}, u32[]{:S(2)}, u32[]{:S(2)}) collective-permute-start(bf16[144,1024]{1,0:T(8,128)(2,1)S(1)} %shard_map.78.refs_1_.refs_11_), channel_id=1, source_target_pairs={{0,8},{1,17},{2,10},{3,19},{4,12},{5,21},{6,14},{7,23},{8,0},{9,25... | collective-permute-start | bytes 884744 | tf_op jit(solution)/shard_map/ppermute | solution.py:40
  22.1 8.0 %collective-permute-start.17 = (bf16[144,1024]{1,0:T(8,128)(2,1)S(1)}, bf16[144,1024]{1,0:T(8,128)(2,1)S(1)}, u32[]{:S(2)}, u32[]{:S(2)}) collective-permute-start(bf16[144,1024]{1,0:T(8,128)(2,1)S(1)} %shard_map.78.refs_1_.refs_11_), channel_id=1, source_target_pairs={{0,16},{1,9},{2,18},{3,11},{4,20},{5,13},{6,22},{7,15},{8,24},{9,1... | collective-permute-start | bytes 884744 | tf_op jit(solution)/shard_map/ppermute | solution.py:40
  23.6 10.0 %collective-permute-start.19 = (bf16[144,1024]{1,0:T(8,128)(2,1)S(1)}, bf16[144,1024]{1,0:T(8,128)(2,1)S(1)}, u32[]{:S(2)}, u32[]{:S(2)}) collective-permute-start(bf16[144,1024]{1,0:T(8,128)(2,1)S(1)} %shard_map.78.refs_1_.refs_11_), channel_id=1, source_target_pairs={{0,1},{1,0},{2,3},{3,2},{4,5},{5,4},{6,7},{7,6},{8,9},{9,8},{10,11... | collective-permute-start | bytes 884744 | tf_op jit(solution)/shard_map/ppermute | solution.py:40
  30.1 8.9 %collective-permute-start.18 = (bf16[144,1024]{1,0:T(8,128)(2,1)S(1)}, bf16[144,1024]{1,0:T(8,128)(2,1)S(1)}, u32[]{:S(2)}, u32[]{:S(2)}) collective-permute-start(bf16[144,1024]{1,0:T(8,128)(2,1)S(1)} %collective-permute-done.16.refs_2_.refs_12_), channel_id=1, source_target_pairs={{0,16},{1,9},{2,18},{3,11},{4,20},{5,13},{6,22},{7,15},{8,24},{9,1... | collective-permute-start | bytes 884744 | tf_op jit(solution)/shard_map/ppermute | solution.py:40
  31.5 8.3 %collective-permute-start.20 = (bf16[144,1024]{1,0:T(8,128)(2,1)S(1)}, bf16[144,1024]{1,0:T(8,128)(2,1)S(1)}, u32[]{:S(2)}, u32[]{:S(2)}) collective-permute-start(bf16[144,1024]{1,0:T(8,128)(2,1)S(1)} %collective-permute-done.16.refs_2_.refs_12_), channel_id=1, source_target_pairs={{0,1},{1,0},{2,3},{3,2},{4,5},{5,4},{6,7},{7,6},{8,9},{9,8},{10,11... | collective-permute-start | bytes 884744 | tf_op jit(solution)/shard_map/ppermute | solution.py:40
  31.5 24.5 %collective-permute-start.7 = (bf16[256,1024]{1,0:T(8,128)(2,1)S(1)}, bf16[256,1024]{1,0:T(8,128)(2,1)}, u32[]{:S(2)}, u32[]{:S(2)}) collective-permute-start(bf16[256,1024]{1,0:T(8,128)(2,1)S(1)} %shard_map.79.refs_1_), channel_id=1, source_target_pairs={{0,8},{1,17},{2,10},{3,19},{4,12},{5,21},{6,14},{7,23},{8,0},{9,25... | collective-permute-start | bytes 1572872 | tf_op jit(solution)/shard_map/ppermute | solution.py:40
  33.0 23.1 %collective-permute-start.8 = (bf16[256,1024]{1,0:T(8,128)(2,1)S(1)}, bf16[256,1024]{1,0:T(8,128)(2,1)}, u32[]{:S(2)}, u32[]{:S(2)}) collective-permute-start(bf16[256,1024]{1,0:T(8,128)(2,1)S(1)} %shard_map.79.refs_1_), channel_id=1, source_target_pairs={{0,16},{1,9},{2,18},{3,11},{4,20},{5,13},{6,22},{7,15},{8,24},{9,1... | collective-permute-start | bytes 1572872 | tf_op jit(solution)/shard_map/ppermute | solution.py:40
  33.6 0.7 copy-start.6
  34.3 7.0 %collective-permute-start.21 = (bf16[144,1024]{1,0:T(8,128)(2,1)S(1)}, bf16[144,1024]{1,0:T(8,128)(2,1)S(1)}, u32[]{:S(2)}, u32[]{:S(2)}) collective-permute-start(bf16[144,1024]{1,0:T(8,128)(2,1)S(1)} %collective-permute-done.17.refs_3_.refs_13_), channel_id=1, source_target_pairs={{0,1},{1,0},{2,3},{3,2},{4,5},{5,4},{6,7},{7,6},{8,9},{9,8},{10,11... | collective-permute-start | bytes 884744 | tf_op jit(solution)/shard_map/ppermute | solution.py:40
  34.3 0.7 copy-start
  39.0 3.0 %collective-permute-start.22 = (bf16[144,1024]{1,0:T(8,128)(2,1)S(1)}, bf16[144,1024]{1,0:T(8,128)(2,1)S(1)}, u32[]{:S(2)}, u32[]{:S(2)}) collective-permute-start(bf16[144,1024]{1,0:T(8,128)(2,1)S(1)} %collective-permute-done.18.refs_4_.refs_14_), channel_id=1, source_target_pairs={{0,1},{1,0},{2,3},{3,2},{4,5},{5,4},{6,7},{7,6},{8,9},{9,8},{10,11... | collective-permute-start | bytes 884744 | tf_op jit(solution)/shard_map/ppermute | solution.py:40
  39.0 0.7 copy-start.3
  39.8 0.7 copy-start.8
  40.5 15.6 %collective-permute-start.2 = (bf16[128,1024]{1,0:T(8,128)(2,1)}, bf16[128,1024]{1,0:T(8,128)(2,1)}, u32[]{:S(2)}, u32[]{:S(2)}) collective-permute-start(bf16[128,1024]{1,0:T(8,128)(2,1)} %refs_0_.1), channel_id=1, source_target_pairs={{0,4},{1,5},{2,6},{3,7},{4,0},{5,1},{6,2},{7,3},{8,12},{9,13},{10,... | collective-permute-start | bytes 786440 | tf_op jit(solution)/shard_map/ppermute | solution.py:40
  41.3 0.7 copy-start.10
  42.0 0.7 copy-start.12
  42.7 1.0 copy-start.1
  43.7 1.0 copy-start.4
  44.7 1.0 copy-start.7
  45.6 1.0 copy-start.9
  46.6 1.0 copy-start.11
  47.6 1.0 copy-start.13
  56.1 15.3 %collective-permute-start.23 = (bf16[256,1024]{1,0:T(8,128)(2,1)}, bf16[256,1024]{1,0:T(8,128)(2,1)}, u32[]{:S(2)}, u32[]{:S(2)}) collective-permute-start(bf16[256,1024]{1,0:T(8,128)(2,1)} %collective-permute-done.7.refs_2_), channel_id=1, source_target_pairs={{0,16},{1,9},{2,18},{3,11},{4,20},{5,13},{6,22},{7,15},{8,24},{9,1... | collective-permute-start | bytes 1572872 | tf_op jit(solution)/shard_map/ppermute | solution.py:40
  60.0 11.3 %collective-permute-start.10 = (bf16[128,1024]{1,0:T(8,128)(2,1)}, bf16[128,1024]{1,0:T(8,128)(2,1)}, u32[]{:S(2)}, u32[]{:S(2)}) collective-permute-start(bf16[128,1024]{1,0:T(8,128)(2,1)} %shard_map.80.refs_1_), channel_id=1, source_target_pairs={{0,16},{1,9},{2,18},{3,11},{4,20},{5,13},{6,22},{7,15},{8,24},{9,1... | collective-permute-start | bytes 786440 | tf_op jit(solution)/shard_map/ppermute | solution.py:40
  60.1 14.0 %collective-permute-start.24 = (bf16[256,1024]{1,0:T(8,128)(2,1)S(1)}, bf16[256,1024]{1,0:T(8,128)(2,1)}, u32[]{:S(2)}, u32[]{:S(2)}) collective-permute-start(bf16[256,1024]{1,0:T(8,128)(2,1)S(1)} %shard_map.79.refs_1_), channel_id=1, source_target_pairs={{0,1},{1,0},{2,3},{3,2},{4,5},{5,4},{6,7},{7,6},{8,9},{9,8},{10,11... | collective-permute-start | bytes 1572872 | tf_op jit(solution)/shard_map/ppermute | solution.py:40
  60.2 11.6 %collective-permute-start.9 = (bf16[128,1024]{1,0:T(8,128)(2,1)}, bf16[128,1024]{1,0:T(8,128)(2,1)}, u32[]{:S(2)}, u32[]{:S(2)}) collective-permute-start(bf16[128,1024]{1,0:T(8,128)(2,1)} %shard_map.80.refs_1_), channel_id=1, source_target_pairs={{0,8},{1,17},{2,10},{3,19},{4,12},{5,21},{6,14},{7,23},{8,0},{9,25... | collective-permute-start | bytes 786440 | tf_op jit(solution)/shard_map/ppermute | solution.py:40
  61.8 12.4 %collective-permute-start.25 = (bf16[256,1024]{1,0:T(8,128)(2,1)}, bf16[256,1024]{1,0:T(8,128)(2,1)}, u32[]{:S(2)}, u32[]{:S(2)}) collective-permute-start(bf16[256,1024]{1,0:T(8,128)(2,1)} %collective-permute-done.7.refs_2_), channel_id=1, source_target_pairs={{0,1},{1,0},{2,3},{3,2},{4,5},{5,4},{6,7},{7,6},{8,9},{9,8},{10,11... | collective-permute-start | bytes 1572872 | tf_op jit(solution)/shard_map/ppermute | solution.py:40
  71.3 3.4 %collective-permute-start.26 = (bf16[256,1024]{1,0:T(8,128)(2,1)}, bf16[256,1024]{1,0:T(8,128)(2,1)}, u32[]{:S(2)}, u32[]{:S(2)}) collective-permute-start(bf16[256,1024]{1,0:T(8,128)(2,1)} %collective-permute-done.8.refs_3_), channel_id=1, source_target_pairs={{0,1},{1,0},{2,3},{3,2},{4,5},{5,4},{6,7},{7,6},{8,9},{9,8},{10,11... | collective-permute-start | bytes 1572872 | tf_op jit(solution)/shard_map/ppermute | solution.py:40
  71.3 7.2 %collective-permute-start.27 = (bf16[256,1024]{1,0:T(8,128)(2,1)}, bf16[256,1024]{1,0:T(8,128)(2,1)}, u32[]{:S(2)}, u32[]{:S(2)}) collective-permute-start(bf16[256,1024]{1,0:T(8,128)(2,1)} %collective-permute-done.23.refs_4_), channel_id=1, source_target_pairs={{0,1},{1,0},{2,3},{3,2},{4,5},{5,4},{6,7},{7,6},{8,9},{9,8},{10,11... | collective-permute-start | bytes 1572872 | tf_op jit(solution)/shard_map/ppermute | solution.py:40
  71.8 6.7 %collective-permute-start.11 = (bf16[128,1024]{1,0:T(8,128)(2,1)}, bf16[128,1024]{1,0:T(8,128)(2,1)}, u32[]{:S(2)}, u32[]{:S(2)}) collective-permute-start(bf16[128,1024]{1,0:T(8,128)(2,1)} %collective-permute-done.9.refs_2_), channel_id=1, source_target_pairs={{0,16},{1,9},{2,18},{3,11},{4,20},{5,13},{6,22},{7,15},{8,24},{9,1... | collective-permute-start | bytes 786440 | tf_op jit(solution)/shard_map/ppermute | solution.py:40
  74.1 19.0 %collective-permute-start.12 = (bf16[128,1024]{1,0:T(8,128)(2,1)}, bf16[128,1024]{1,0:T(8,128)(2,1)S(1)}, u32[]{:S(2)}, u32[]{:S(2)}) collective-permute-start(bf16[128,1024]{1,0:T(8,128)(2,1)} %shard_map.80.refs_1_), channel_id=1, source_target_pairs={{0,1},{1,0},{2,3},{3,2},{4,5},{5,4},{6,7},{7,6},{8,9},{9,8},{10,11... | collective-permute-start | bytes 786440 | tf_op jit(solution)/shard_map/ppermute | solution.py:40
  74.2 18.9 %collective-permute-start.13 = (bf16[128,1024]{1,0:T(8,128)(2,1)}, bf16[128,1024]{1,0:T(8,128)(2,1)S(1)}, u32[]{:S(2)}, u32[]{:S(2)}) collective-permute-start(bf16[128,1024]{1,0:T(8,128)(2,1)} %collective-permute-done.9.refs_2_), channel_id=1, source_target_pairs={{0,1},{1,0},{2,3},{3,2},{4,5},{5,4},{6,7},{7,6},{8,9},{9,8},{10,11... | collective-permute-start | bytes 786440 | tf_op jit(solution)/shard_map/ppermute | solution.py:40
  74.7 18.4 %collective-permute-start.14 = (bf16[128,1024]{1,0:T(8,128)(2,1)}, bf16[128,1024]{1,0:T(8,128)(2,1)S(1)}, u32[]{:S(2)}, u32[]{:S(2)}) collective-permute-start(bf16[128,1024]{1,0:T(8,128)(2,1)} %collective-permute-done.10.refs_3_), channel_id=1, source_target_pairs={{0,1},{1,0},{2,3},{3,2},{4,5},{5,4},{6,7},{7,6},{8,9},{9,8},{10,11... | collective-permute-start | bytes 786440 | tf_op jit(solution)/shard_map/ppermute | solution.py:40
  78.5 14.6 %collective-permute-start.15 = (bf16[128,1024]{1,0:T(8,128)(2,1)}, bf16[128,1024]{1,0:T(8,128)(2,1)S(1)}, u32[]{:S(2)}, u32[]{:S(2)}) collective-permute-start(bf16[128,1024]{1,0:T(8,128)(2,1)} %collective-permute-done.11.refs_4_), channel_id=1, source_target_pairs={{0,1},{1,0},{2,3},{3,2},{4,5},{5,4},{6,7},{7,6},{8,9},{9,8},{10,11... | collective-permute-start | bytes 786440 | tf_op jit(solution)/shard_map/ppermute | solution.py:40
  85.8 7.4 %copy-start.2 = (bf16[144,1024]{1,0:T(8,128)(2,1)S(1)}, bf16[144,1024]{1,0:T(8,128)(2,1)}, u32[]{:S(2)}) copy-start(bf16[144,1024]{1,0:T(8,128)(2,1)} %copy-done) | copy-start | bytes 884740
  85.8 7.4 %copy-start.5 = (bf16[144,1024]{1,0:T(8,128)(2,1)S(1)}, bf16[144,1024]{1,0:T(8,128)(2,1)}, u32[]{:S(2)}) copy-start(bf16[144,1024]{1,0:T(8,128)(2,1)} %copy-done.3) | copy-start | bytes 884740
  93.1 19.8 %copy-start.14 = (f32[128]{0:T(128)S(1)}, f32[128]{0:T(128)}, u32[]{:S(2)}) copy-start(f32[128]{0:T(128)} %param.10) | copy-start | bytes 1540
  100.9 11.9 %all-to-all-start = ((f32[32,3,128]{2,1,0:T(4,128)}), f32[32,3,128]{2,1,0:T(4,128)S(1)}, u32[]{:S(2)}, u32[]{:S(2)}) async-start(f32[32,3,128]{2,1,0:T(4,128)} %bitcast.14), calls=%async_computation | async-start | bytes 131072 | tf_op jit(solution)/shard_map/all_to_all | solution.py:318
